TPU v7x, 32 devices: a whole 2x2x4 slice. The times are simulated.
32 devices in a mesh: expert: 8 (over y, x, core), hidden: 4 (over z).
Axes of the slice: x: 2, y: 2, z: 4, core: 2. Of those that a mesh axis runs over, the one named last changes fastest.
Arguments:
- tokens: bfloat16 [6272, 768], P(('expert', 'hidden')), may hold values from -512 to 512
- out_grad: bfloat16 [6272, 768], P(('expert', 'hidden')), may hold values from -12 to 12
- slot_router: bfloat16 [768, 32], replicated, may hold values from -0.5 to 0.5
- weight_in: bfloat16 [16, 768, 3072], P('expert', None, 'hidden'), may hold values from -0.21875 to 0.21875
- weight_out: bfloat16 [16, 3072, 768], P('expert', 'hidden'), may hold values from -0.109375 to 0.109375
Outputs:
- token_grad: bfloat16 [6272, 768], P(('expert', 'hidden'))
- router_grad: float32 [768, 32], P('hidden', 'expert')
- weight_in_grad: bfloat16 [16, 768, 3072], P('expert', None, 'hidden')
- weight_out_grad: bfloat16 [16, 3072, 768], P('expert', 'hidden')
All inputs are finite; a program needn't handle non-finite values.
Results may differ from a plain program's by a relative error of at most 0.019.
Values may be sent and summed in bfloat16 or wider, within the bound.
No kernel may reach another device: no remote copies, remote signals or barrier semaphores. Data moves between devices by JAX's collectives and lax.ppermute only.
A program may use at most 64 MiB of HBM per device.

v0:
```python
import jax
import jax.numpy as jnp
from jax import lax
from jax.sharding import PartitionSpec as P

D = 768
SLOTS = 2
TOK = 196


def gelu_value(values):
    return 0.5 * values * (1.0 + lax.erf(values * 0.7071067811865476))


def gelu_slope(values):
    return (
        0.5 * (1.0 + lax.erf(values * 0.7071067811865476))
        + values * jnp.exp(-0.5 * values * values) * 0.3989422804014327
    )


def to_experts(stacked_slots):
    crossed = lax.all_to_all(stacked_slots, "expert", split_axis=2, concat_axis=0, tiled=True)
    arrived = lax.all_gather(crossed, "hidden", axis=0, tiled=True)
    return arrived


def to_owners(partials):
    rounded = lax.optimization_barrier(partials.astype(jnp.bfloat16))
    summed = lax.psum_scatter(
        rounded.astype(jnp.float32).astype(jnp.bfloat16), "hidden", scatter_dimension=0, tiled=True
    )
    result = lax.all_to_all(summed, "expert", split_axis=0, concat_axis=2, tiled=True)
    return result


def per_device(tokens, out_grad, slot_router, weight_in, weight_out):
    images = tokens.shape[0] // TOK
    local_experts = weight_in.shape[0]
    inputs = tokens.reshape(images, TOK, D)
    out_grads = out_grad.reshape(images, TOK, D)
    logits = jnp.einsum("btd,dc->btc", inputs, slot_router, preferred_element_type=jnp.float32)
    dispatch = jax.nn.softmax(logits, axis=1)
    combine = jax.nn.softmax(logits, axis=2)
    dispatch16 = dispatch.astype(jnp.bfloat16)
    combine16 = combine.astype(jnp.bfloat16)
    slot_in = jnp.einsum(
        "btc,btd->bcd", dispatch16, inputs, preferred_element_type=jnp.float32
    ).astype(jnp.bfloat16)
    slot_grad = jnp.einsum(
        "btc,btd->bcd", combine16, out_grads, preferred_element_type=jnp.float32
    ).astype(jnp.bfloat16)
    arrived = to_experts(slot_in[:, None])
    received = arrived[:, 0]
    row_count = received.shape[0]
    slot_inputs = received.reshape(row_count, local_experts, SLOTS, D)
    pre_act = jnp.einsum(
        "resd,edf->resf", slot_inputs, weight_in, preferred_element_type=jnp.float32
    )
    activated = gelu_value(pre_act).astype(jnp.bfloat16)
    partial_value = jnp.einsum(
        "resf,efd->resd", activated, weight_out, preferred_element_type=jnp.float32
    )
    slot_inputs, pre_act, activated, forward_part = (
        slot_inputs,
        pre_act,
        activated,
        partial_value.reshape(row_count, 1, local_experts * SLOTS, D),
    )
    slot_out = to_owners(forward_part)[:, 0]
    arrived_grad = to_experts(slot_grad[:, None])
    received_grad = arrived_grad[:, 0]
    row_count = received_grad.shape[0]
    slot_grads = received_grad.reshape(row_count, local_experts, SLOTS, D)
    d_act = jnp.einsum("resd,efd->resf", slot_grads, weight_out, preferred_element_type=jnp.float32)
    d_pre = (d_act * gelu_slope(pre_act)).astype(jnp.bfloat16)
    grad_second = jnp.einsum(
        "resf,resd->efd", activated, slot_grads, preferred_element_type=jnp.float32
    ).astype(jnp.bfloat16)
    grad_first = jnp.einsum(
        "resd,resf->edf", slot_inputs, d_pre, preferred_element_type=jnp.float32
    ).astype(jnp.bfloat16)
    partial_value = jnp.einsum(
        "resf,edf->resd", d_pre, weight_in, preferred_element_type=jnp.float32
    )
    backward_part = partial_value.reshape(row_count, 1, local_experts * SLOTS, D)
    slot_in_grad = to_owners(backward_part)[:, 0]
    d_combine = jnp.einsum("btd,bcd->btc", out_grads, slot_out, preferred_element_type=jnp.float32)
    d_dispatch = jnp.einsum(
        "btd,bcd->btc", inputs, slot_in_grad, preferred_element_type=jnp.float32
    )
    from_combine = combine * (d_combine - jnp.sum(combine * d_combine, axis=2, keepdims=True))
    from_dispatch = dispatch * (d_dispatch - jnp.sum(dispatch * d_dispatch, axis=1, keepdims=True))
    d_logits = (from_combine + from_dispatch).astype(jnp.bfloat16)
    token_grad = (
        jnp.einsum("btc,bcd->btd", dispatch16, slot_in_grad, preferred_element_type=jnp.float32)
        + jnp.einsum("btc,dc->btd", d_logits, slot_router, preferred_element_type=jnp.float32)
    ).astype(jnp.bfloat16)
    router_term = jnp.einsum("btd,btc->dc", inputs, d_logits, preferred_element_type=jnp.float32)
    column_part = lax.psum_scatter(router_term, "expert", scatter_dimension=1, tiled=True)
    router_grad = lax.psum_scatter(column_part, "hidden", scatter_dimension=0, tiled=True)
    return (token_grad.reshape(images * TOK, D), router_grad, grad_first, grad_second)


def solution(mesh):
    return jax.shard_map(
        per_device,
        mesh=mesh,
        in_specs=(
            P(("expert", "hidden"), None),
            P(("expert", "hidden"), None),
            P(),
            P("expert", None, "hidden"),
            P("expert", "hidden", None),
        ),
        out_specs=(
            P(("expert", "hidden"), None),
            P("hidden", "expert"),
            P("expert", None, "hidden"),
            P("expert", "hidden", None),
        ),
        check_vma=False,
    )
```

profile of v0, /device:TPU:0, one launch (start us, length us, event | category | flops | bytes accessed | tf_op | source)
XLA Modules:
  0.0 192.4 jit_solution(2502816265532646498)
XLA Ops:
  7.2 1.5 fusion.44
  8.8 1.1 fusion.27
  10.6 0.9 reduce.16
  12.2 5.2 %all-to-all-start = ((bf16[8,2,1536]{2,1,0:T(2,128)(2,1)}), bf16[8,2,1536]{2,1,0:T(2,128)(2,1)S(1)}, u32[]{:S(2)}, u32[]{:S(2)}) async-start(bf16[8,2,1536]{2,1,0:T(2,128)(2,1)} %reshape.160), calls=%async_computation | async-start | bytes 98304 | tf_op jit(solution)/shard_map/all_to_all | solution.py:23
  17.3 1.2 fusion.28
  18.6 0.9 reduce.17
  20.2 2.1 %all-to-all-done = bf16[8,2,1536]{2,1,0:T(2,128)(2,1)S(1)} async-done(((bf16[8,2,1536]{2,1,0:T(2,128)(2,1)}), bf16[8,2,1536]{2,1,0:T(2,128)(2,1)S(1)}, u32[]{:S(2)}, u32[]{:S(2)}) %all-to-all-start) | async-done | bytes 49184 | tf_op jit(solution)/shard_map/all_to_all | solution.py:23
  22.3 3.3 %all-to-all-start.1 = ((bf16[8,2,1536]{2,1,0:T(2,128)(2,1)}), bf16[8,2,1536]{2,1,0:T(2,128)(2,1)S(1)}, u32[]{:S(2)}, u32[]{:S(2)}) async-start(bf16[8,2,1536]{2,1,0:T(2,128)(2,1)} %reshape.162), calls=%async_computation.1 | async-start | bytes 98304 | tf_op jit(solution)/shard_map/all_to_all | solution.py:23
  26.0 4.5 %all-to-all-done.1 = bf16[8,2,1536]{2,1,0:T(2,128)(2,1)S(1)} async-done(((bf16[8,2,1536]{2,1,0:T(2,128)(2,1)}), bf16[8,2,1536]{2,1,0:T(2,128)(2,1)S(1)}, u32[]{:S(2)}, u32[]{:S(2)}) %all-to-all-start.1) | async-done | bytes 49184 | tf_op jit(solution)/shard_map/all_to_all | solution.py:23
  30.8 14.1 %all_gather.7 = bf16[32,1,4,768]{3,2,1,0:T(4,128)(2,1)S(1)} all-gather(bf16[8,1,4,768]{3,2,1,0:T(4,128)(2,1)S(1)} %bitcast.120), channel_id=1, replica_groups=mesh['expert'=8,'hidden'=4] {'hidden'}, dimensions={0}, use_global_device_ids=true | all-gather | bytes 245760 | tf_op jit(solution)/shard_map/all_gather | solution.py:24
  45.0 14.0 %all_gather.6 = bf16[32,1,4,768]{3,2,1,0:T(4,128)(2,1)S(1)} all-gather(bf16[8,1,4,768]{3,2,1,0:T(4,128)(2,1)S(1)} %bitcast.119), channel_id=1, replica_groups=mesh['expert'=8,'hidden'=4] {'hidden'}, dimensions={0}, use_global_device_ids=true | all-gather | bytes 245760 | tf_op jit(solution)/shard_map/all_gather | solution.py:24
  59.5 0.8 fusion.24
  60.4 0.8 fusion.21
  61.4 0.7 copy.49
  63.4 2.2 %fusion.18 = bf16[2,32,2,768]{3,1,2,0:T(8,128)(2,1)S(1)} fusion(bf16[2,768,768]{2,1,0:T(8,128)(2,1)} %param.9, f32[32,2,2,768]{3,0,2,1:T(8,128)S(1)} %fusion.12), kind=kOutput, calls=%fused_computation.15 | convolution fusion | flops 151584768 | bytes 2949120 | tf_op jit(solution)/shard_map/resf,efd->resd/dot_general | solution.py:61
  65.7 0.7 copy.50
  66.5 2.2 %bitcast_convert_fusion = bf16[2,768,768]{2,1,0:T(8,128)(2,1)} fusion(bf16[32,2,2,768]{3,0,2,1:T(8,128)(2,1)S(1)} %bitcast.108, f32[32,2,2,768]{3,0,2,1:T(8,128)S(1)} %fusion.12), kind=kOutput, calls=%fused_computation | convolution fusion | flops 152666112 | bytes 2949120 | tf_op jit(solution)/shard_map/resf,resd->efd/dot_general | solution.py:77
  68.7 12.2 %reduce-scatter.12.cloned.1.call-done = bf16[8,3072]{1,0:T(8,128)(2,1)} async-done(((bf16[32,3072]{1,0:T(8,128)(2,1)}), bf16[8,3072]{1,0:T(8,128)(2,1)}) %reduce-scatter.12.cloned.1.call-update) | async-done | bytes 49168
  80.9 1.4 reshape.152
  82.4 3.7 %all-to-all-start.2 = ((bf16[8,1,4,768]{3,2,1,0:T(4,128)(2,1)}), bf16[8,1,4,768]{3,2,1,0:T(4,128)(2,1)S(1)}, u32[]{:S(2)}, u32[]{:S(2)}) async-start(bf16[8,1,4,768]{3,2,1,0:T(4,128)(2,1)} %reshape.152), calls=%async_computation.2 | async-start | bytes 98304 | tf_op jit(solution)/shard_map/all_to_all | solution.py:33
  86.0 2.2 %bitcast_convert_fusion.1 = bf16[2,768,768]{2,1,0:T(8,128)(2,1)} fusion(bf16[32,2,2,768]{3,0,2,1:T(8,128)(2,1)S(1)} %bitcast.110, bf16[32,2,2,768]{3,0,2,1:T(8,128)(2,1)S(1)} %fusion.24), kind=kOutput, calls=%fused_computation.1 | convolution fusion | flops 152174592 | bytes 2752512 | tf_op jit(solution)/shard_map/resd,resf->edf/dot_general | solution.py:80
  88.3 12.6 %reduce-scatter.14.cloned.1.call-done = bf16[8,3072]{1,0:T(8,128)(2,1)} async-done(((bf16[32,3072]{1,0:T(8,128)(2,1)}), bf16[8,3072]{1,0:T(8,128)(2,1)}) %reduce-scatter.14.cloned.1.call-update) | async-done | bytes 49168
  100.9 1.4 reshape.154
  102.3 3.7 %all-to-all-start.3 = ((bf16[8,1,4,768]{3,2,1,0:T(4,128)(2,1)}), bf16[8,1,4,768]{3,2,1,0:T(4,128)(2,1)S(1)}, u32[]{:S(2)}, u32[]{:S(2)}) async-start(bf16[8,1,4,768]{3,2,1,0:T(4,128)(2,1)} %reshape.154), calls=%async_computation.3 | async-start | bytes 98304 | tf_op jit(solution)/shard_map/all_to_all | solution.py:33
  106.2 4.7 %all-to-all-done.3 = bf16[8,1,4,768]{3,2,1,0:T(4,128)(2,1)S(1)} async-done(((bf16[8,1,4,768]{3,2,1,0:T(4,128)(2,1)}), bf16[8,1,4,768]{3,2,1,0:T(4,128)(2,1)S(1)}, u32[]{:S(2)}, u32[]{:S(2)}) %all-to-all-start.3) | async-done | bytes 49184 | tf_op jit(solution)/shard_map/all_to_all | solution.py:33
  111.2 0.9 convolution_bitcast_fusion
  112.5 48.2 %all-reduce.3.cloned.1.call-done = f32[768,32]{0,1:T(8,128)} async-done(((f32[768,32]{0,1:T(8,128)}), f32[768,32]{0,1:T(8,128)}) %all-reduce.3.cloned.1.call-update) | async-done | bytes 98320
  160.7 0.7 constant_dynamic-slice_fusion
  161.4 0.9 copy.43
  162.4 1.1 fusion.8
  163.5 20.9 %reduce-scatter.16.cloned.1.call-done = f32[192,4]{1,0:T(8,128)} async-done(((f32[768,4]{1,0:T(8,128)}), f32[192,4]{1,0:T(8,128)}) %reduce-scatter.16.cloned.1.call-update) | async-done | bytes 3088
  184.3 1.6 copy.44
  (44 shorter events, 5.4 us)
Async XLA Ops:
  7.2 51.8 %copy-start = (bf16[2,768,768]{2,1,0:T(8,128)(2,1)S(1)}, bf16[2,768,768]{2,1,0:T(8,128)(2,1)}, u32[]{:S(2)}) copy-start(bf16[2,768,768]{2,1,0:T(8,128)(2,1)} %param.8) | copy-start | bytes 7077892
  12.2 10.1 %all-to-all-start = ((bf16[8,2,1536]{2,1,0:T(2,128)(2,1)}), bf16[8,2,1536]{2,1,0:T(2,128)(2,1)S(1)}, u32[]{:S(2)}, u32[]{:S(2)}) async-start(bf16[8,2,1536]{2,1,0:T(2,128)(2,1)} %reshape.160), calls=%async_computation | async-start | bytes 98304 | tf_op jit(solution)/shard_map/all_to_all | solution.py:23
  22.3 8.2 %all-to-all-start.1 = ((bf16[8,2,1536]{2,1,0:T(2,128)(2,1)}), bf16[8,2,1536]{2,1,0:T(2,128)(2,1)S(1)}, u32[]{:S(2)}, u32[]{:S(2)}) async-start(bf16[8,2,1536]{2,1,0:T(2,128)(2,1)} %reshape.162), calls=%async_computation.1 | async-start | bytes 98304 | tf_op jit(solution)/shard_map/all_to_all | solution.py:23
  25.6 55.3 %reduce-scatter.12.cloned.1.call-start = ((), (), s32[]{:S(2)}) async-start(), calls=%async_computation.7 | async-start | bytes 245760
  30.8 28.7 %copy-start.1 = (bf16[2,768,768]{2,1,0:T(8,128)(2,1)S(1)}, bf16[2,768,768]{2,1,0:T(8,128)(2,1)}, u32[]{:S(2)}) copy-start(bf16[2,768,768]{2,1,0:T(8,128)(2,1)} %param.9) | copy-start | bytes 7077892
  60.4 1.8 copy-start.5
  62.1 38.8 %reduce-scatter.14.cloned.1.call-start = ((), (), s32[]{:S(2)}) async-start(), calls=%async_computation.8 | async-start | bytes 245760
  68.7 37.4 %copy-start.2 = (bf16[196,768]{1,0:T(8,128)(2,1)S(1)}, bf16[196,768]{1,0:T(8,128)(2,1)}, u32[]{:S(2)}) copy-start(bf16[196,768]{1,0:T(8,128)(2,1)} %param.5) | copy-start | bytes 903172
  68.7 42.2 %copy-start.3 = (bf16[196,768]{1,0:T(8,128)(2,1)S(1)}, bf16[196,768]{1,0:T(8,128)(2,1)}, u32[]{:S(2)}) copy-start(bf16[196,768]{1,0:T(8,128)(2,1)} %param.6) | copy-start | bytes 903172
  82.4 20.0 %all-to-all-start.2 = ((bf16[8,1,4,768]{3,2,1,0:T(4,128)(2,1)}), bf16[8,1,4,768]{3,2,1,0:T(4,128)(2,1)S(1)}, u32[]{:S(2)}, u32[]{:S(2)}) async-start(bf16[8,1,4,768]{3,2,1,0:T(4,128)(2,1)} %reshape.152), calls=%async_computation.2 | async-start | bytes 98304 | tf_op jit(solution)/shard_map/all_to_all | solution.py:33
  88.3 74.1 %copy-start.4 = (bf16[768,32]{0,1:T(8,128)(2,1)S(1)}, bf16[768,32]{0,1:T(8,128)(2,1)}, u32[]{:S(2)}) copy-start(bf16[768,32]{0,1:T(8,128)(2,1)} %param.7) | copy-start | bytes 147460
  102.3 8.6 %all-to-all-start.3 = ((bf16[8,1,4,768]{3,2,1,0:T(4,128)(2,1)}), bf16[8,1,4,768]{3,2,1,0:T(4,128)(2,1)S(1)}, u32[]{:S(2)}, u32[]{:S(2)}) async-start(bf16[8,1,4,768]{3,2,1,0:T(4,128)(2,1)} %reshape.154), calls=%async_computation.3 | async-start | bytes 98304 | tf_op jit(solution)/shard_map/all_to_all | solution.py:33
  106.0 54.7 %all-reduce.3.cloned.1.call-start = ((), (), s32[]{:S(2)}) async-start(), calls=%async_computation.10 | async-start | bytes 196608
  112.1 72.2 %reduce-scatter.16.cloned.1.call-start = ((), (), s32[]{:S(2)}) async-start(), calls=%async_computation.9 | async-start | bytes 491520
Sparse Core Ops, SparseCore 0:
  62.2 18.6 reduce-scatter.11
  83.3 17.5 reduce-scatter.13
  112.2 48.4 all-reduce.2
  162.9 21.3 reduce-scatter.15
where the time goes:
time: 193 us; the launch traced here: 192 us
  waiting for transfers between devices  105 us (54%)
  blocking collectives  28.1 us (15%)
  starting transfers between devices  16 us (8%)
  matrix products  15.3 us (8%)
  between operations  14.6 us (8%)
  local copies, waits for them, and re-layouts  11.2 us (6%)
  other arithmetic  2.02 us (1%)
    unnamed x8, waiting for transfers between devices  93.9 us
    all_gather x2, blocking collectives, to_experts(): arrived = lax.all_gather(crossed, 'hidden', axis=0, tiled=True)  28.1 us
    all_to_all x2, starting transfers between devices, to_experts(): lax.all_to_all(stacked_slots, 'expert', split_axis=2, concat_axis=0, tile...  8.52 us
    unnamed x25, local copies, waits for them, and re-layouts  7.46 us
    all_to_all x2, starting transfers between devices, to_owners(): lax.all_to_all(summed, 'expert', split_axis=0, concat_axis=2, tiled=True)  7.34 us
    all_to_all x2, waiting for transfers between devices, to_experts(): lax.all_to_all(stacked_slots, 'expert', split_axis=2, concat_axis=0, tile...  6.55 us
    all_to_all x2, waiting for transfers between devices, to_owners(): lax.all_to_all(summed, 'expert', split_axis=0, concat_axis=2, tiled=True)  4.68 us
  transfers between devices with their start and end apart: 8, of which 7 were waited for; matrix products, arithmetic and copies ran while one was open for 8% of the time, Pallas kernels for 0%

commit v1 on v0

v1 whole, which is shorter than its diff:
```python
import jax
import jax.numpy as jnp
from jax import lax
from jax.sharding import PartitionSpec as P

SLOTS = 2
TOK = 196
BOTH = ("expert", "hidden")


def gelu_value(values):
    return 0.5 * values * (1.0 + lax.erf(values * 0.7071067811865476))


def gelu_slope(values):
    return (
        0.5 * (1.0 + lax.erf(values * 0.7071067811865476))
        + values * jnp.exp(-0.5 * values * values) * 0.3989422804014327
    )


def exchange(blocks):
    return lax.all_to_all(blocks, BOTH, split_axis=0, concat_axis=0, tiled=True)


def per_device(n_expert, n_hidden, tokens, out_grad, slot_router, weight_in, weight_out):
    f32, bf16 = jnp.float32, jnp.bfloat16
    width = tokens.shape[1]
    images = tokens.shape[0] // TOK
    local_experts = weight_in.shape[0]
    local_slots = local_experts * SLOTS
    devices = n_expert * n_hidden
    inputs = tokens.reshape(images, TOK, width)
    out_grads = out_grad.reshape(images, TOK, width)
    logits = jnp.einsum("btd,dc->btc", inputs, slot_router, preferred_element_type=f32)
    dispatch = jax.nn.softmax(logits, axis=1)
    combine = jax.nn.softmax(logits, axis=2)
    dispatch16 = dispatch.astype(bf16)
    combine16 = combine.astype(bf16)
    slot_in = jnp.einsum("btc,btd->bcd", dispatch16, inputs, preferred_element_type=f32)
    slot_grad = jnp.einsum("btc,btd->bcd", combine16, out_grads, preferred_element_type=f32)
    slots = jnp.stack([slot_in.astype(bf16), slot_grad.astype(bf16)])
    slots = slots.reshape(2, images, n_expert, local_slots, width).transpose(2, 0, 1, 3, 4)
    sent = jnp.broadcast_to(slots[:, None], (n_expert, n_hidden) + slots.shape[1:])
    received = exchange(sent.reshape(devices, 2 * images * local_slots, width))
    received = received.reshape(devices, 2, images, local_experts, SLOTS, width)
    received = received.transpose(1, 3, 0, 2, 4, 5)
    rows = devices * images * SLOTS
    slot_inputs = received[0].reshape(local_experts, rows, width)
    slot_grads = received[1].reshape(local_experts, rows, width)
    pre_act = jnp.einsum("erd,edf->erf", slot_inputs, weight_in, preferred_element_type=f32)
    activated = gelu_value(pre_act).astype(bf16)
    forward = jnp.einsum("erf,efd->erd", activated, weight_out, preferred_element_type=f32)
    d_act = jnp.einsum("erd,efd->erf", slot_grads, weight_out, preferred_element_type=f32)
    d_pre = (d_act * gelu_slope(pre_act)).astype(bf16)
    backward = jnp.einsum("erf,edf->erd", d_pre, weight_in, preferred_element_type=f32)
    partials = jnp.stack([forward.astype(bf16), backward.astype(bf16)])
    partials = partials.reshape(2, local_experts, devices, images, SLOTS, width)
    partials = partials.transpose(2, 0, 3, 1, 4, 5)
    back = exchange(partials.reshape(devices, 2 * images * local_slots, width))
    grad_second = jnp.einsum("erf,erd->efd", activated, slot_grads, preferred_element_type=f32)
    grad_first = jnp.einsum("erd,erf->edf", slot_inputs, d_pre, preferred_element_type=f32)
    back = back.reshape(n_expert, n_hidden, 2, images, local_slots, width)
    summed = jnp.sum(back.astype(f32), axis=1).astype(bf16).transpose(1, 2, 0, 3, 4)
    summed = summed.reshape(2, images, n_expert * local_slots, width)
    slot_out, slot_in_grad = summed[0], summed[1]
    d_combine = jnp.einsum("btd,bcd->btc", out_grads, slot_out, preferred_element_type=f32)
    d_dispatch = jnp.einsum("btd,bcd->btc", inputs, slot_in_grad, preferred_element_type=f32)
    from_combine = combine * (d_combine - jnp.sum(combine * d_combine, axis=2, keepdims=True))
    from_dispatch = dispatch * (d_dispatch - jnp.sum(dispatch * d_dispatch, axis=1, keepdims=True))
    d_logits = (from_combine + from_dispatch).astype(bf16)
    token_grad = (
        jnp.einsum("btc,bcd->btd", dispatch16, slot_in_grad, preferred_element_type=f32)
        + jnp.einsum("btc,dc->btd", d_logits, slot_router, preferred_element_type=f32)
    ).astype(bf16)
    router_term = jnp.einsum("btc,btd->cd", d_logits, inputs, preferred_element_type=f32)
    router_term = router_term.reshape(n_expert, local_slots, n_hidden, width // n_hidden)
    router_term = router_term.transpose(0, 2, 1, 3)
    router_parts = exchange(router_term.reshape(devices, local_slots, width // n_hidden))
    router_grad = jnp.sum(router_parts, axis=0).T
    return (
        token_grad.reshape(images * TOK, width),
        router_grad,
        grad_first.astype(bf16),
        grad_second.astype(bf16),
    )


def solution(mesh):
    def run(*arrays):
        return per_device(mesh.shape["expert"], mesh.shape["hidden"], *arrays)

    return jax.shard_map(
        run,
        mesh=mesh,
        in_specs=(
            P(BOTH, None),
            P(BOTH, None),
            P(),
            P("expert", None, "hidden"),
            P("expert", "hidden", None),
        ),
        out_specs=(
            P(BOTH, None),
            P("hidden", "expert"),
            P("expert", None, "hidden"),
            P("expert", "hidden", None),
        ),
        check_vma=False,
    )
```

time: 193 us -> 77.8 us (0.40)
  waiting for transfers between devices: 105 us -> 12 us
  between operations: 14.6 us -> 0.93 us
  blocking collectives: 28.1 us -> 18.9 us
  starting transfers between devices: 16 us -> 7.83 us
  local copies, waits for them, and re-layouts: 11.2 us -> 15 us
  matrix products: 15.3 us -> 18.9 us
    unnamed x8 -> x0, waiting for transfers between devices: 93.9 us -> none
    all_gather x2 -> x0, blocking collectives: 28.1 us -> none  [to_experts(): arrived = lax.all_gather(crossed, 'hidden', axis=0, tiled=True)]
    all_to_all x0 -> x1, blocking collectives: none -> 18.9 us  [exchange(): return lax.all_to_all(blocks, BOTH, split_axis=0, concat_axis=0, tiled=True)]
    all_to_all x4 -> x2, starting transfers between devices: 15.9 us -> 7.83 us  [exchange(): return lax.all_to_all(blocks, BOTH, split_axis=0, concat_axis=0, tiled=True)]
    another operation x2 -> x10, local copies, waits for them, and re-layouts: 0.04 us -> 6.85 us  [the longest x4 5.97 us: per_device(): partials = jnp.stack([forward.astype(bf16), backward.astype(bf16)])]
    unnamed x25 -> x21, local copies, waits for them, and re-layouts: 7.46 us -> 2.19 us
    dot_general x13, matrix products: 15 us -> 18.5 us  [the longest x1 3.16 us: per_device(): jnp.einsum('erd,erf->edf', slot_inputs, d_pre, preferred_element_type=f32)]
    reduce_scatter x2 -> x0, local copies, waits for them, and re-layouts: 2.88 us -> none  [to_owners(): lax.psum_scatter(rounded.astype(jnp.float32).astype(jnp.bfloat16), 'hidde...]
  transfers between devices with their start and end apart: 8 -> 2, of which waited for: 7 -> 2; matrix products, arithmetic and copies ran while one was open for 8% -> 11% of each run, Pallas kernels for 0% -> 0%
where the time goes in v1:
time: 77.8 us; the launch traced here: 77 us
  matrix products  18.9 us (24%)
  blocking collectives  18.9 us (24%)
  local copies, waits for them, and re-layouts  15 us (19%)
  waiting for transfers between devices  12 us (15%)
  starting transfers between devices  7.83 us (10%)
  other arithmetic  3.51 us (5%)
  between operations  0.93 us (1%)
    all_to_all x1, blocking collectives, exchange(): return lax.all_to_all(blocks, BOTH, split_axis=0, concat_axis=0, tiled=True)  18.9 us
    all_to_all x2, waiting for transfers between devices, exchange(): return lax.all_to_all(blocks, BOTH, split_axis=0, concat_axis=0, tiled=True)  12 us
    all_to_all x2, starting transfers between devices, exchange(): return lax.all_to_all(blocks, BOTH, split_axis=0, concat_axis=0, tiled=True)  7.83 us
    another operation x4, local copies, waits for them, and re-layouts, per_device(): partials = jnp.stack([forward.astype(bf16), backward.astype(bf16)])  5.97 us
    dot_general x1, matrix products, per_device(): jnp.einsum('erd,erf->edf', slot_inputs, d_pre, preferred_element_type=f32)  3.16 us
    dot_general x1, matrix products, per_device(): jnp.einsum('erf,erd->efd', activated, slot_grads, preferred_element_type=...  2.23 us
    dot_general x1, matrix products, per_device(): jnp.einsum('erd,edf->erf', slot_inputs, weight_in, preferred_element_type...  2.2 us
    unnamed x21, local copies, waits for them, and re-layouts  2.19 us
  transfers between devices with their start and end apart: 2, of which 2 were waited for; matrix products, arithmetic and copies ran while one was open for 11% of the time, Pallas kernels for 0%

profile of v1, /device:TPU:0, one launch (start us, length us, event | category | flops | bytes accessed | tf_op | source)
XLA Modules:
  0.0 77.0 jit_solution(10730586466129917806)
XLA Ops:
  0.6 1.5 %fusion.31 = (f32[32]{0:T(128)S(1)}, f32[196]{0:T(256)S(1)}, f32[196,32]{0,1:T(8,128)S(1)}) fusion(bf16[196,768]{1,0:T(8,128)(2,1)} %param.5, bf16[768,32]{0,1:T(8,128)(2,1)} %param.7), kind=kOutput, calls=%fused_computation.48 | convolution fusion | flops 9646108 | bytes 376208 | tf_op jit(solution)/shard_map/btd,dc->btc/dot_general | solution.py:35
  2.3 1.1 %convolution_convert_fusion.4 = bf16[32,768]{1,0:T(8,128)(2,1)S(1)} fusion(bf16[196,768]{1,0:T(8,128)(2,1)} %param.6, f32[196,32]{0,1:T(8,128)S(1)} %get-tuple-element.14, f32[196]{0:T(256)S(1)} %get-tuple-element.7, f32[196]{0:T(256)S(1)} %get-tuple-element.9), kind=kOutput, calls=%fused_computation.9 | convolution fusion | flops 9677184 | bytes 376864 | tf_op jit(solution)/shard_map/btc,btd->bcd/dot_general | solution.py:41
  3.5 1.2 %convolution_convert_fusion.5 = bf16[32,768]{1,0:T(8,128)(2,1)S(1)} fusion(bf16[196,768]{1,0:T(8,128)(2,1)} %param.5, f32[196,32]{0,1:T(8,128)S(1)} %get-tuple-element.14, f32[32]{0:T(128)S(1)} %get-tuple-element.6, f32[32]{0:T(128)S(1)} %get-tuple-element.8), kind=kOutput, calls=%fused_computation.10 | convolution fusion | flops 9677184 | bytes 375552 | tf_op jit(solution)/shard_map/btc,btd->bcd/dot_general | solution.py:40
  5.1 18.9 %all_to_all.15 = bf16[32,8,768]{2,1,0:T(8,128)(2,1)S(1)} all-to-all(bf16[32,8,768]{2,1,0:T(8,128)(2,1)S(1)} %reshape.140), channel_id=1, replica_groups=mesh['expert'=8,'hidden'=4] {'expert','hidden'}, dimensions={0} | all-to-all | bytes 786432 | tf_op jit(solution)/shard_map/all_to_all | solution.py:23
  24.7 2.2 %fusion.34 = f32[2,64,768]{2,1,0:T(8,128)S(1)} fusion(bf16[2,64,768]{2,1,0:T(8,128)(2,1)S(1)} %reshape_squeeze.6, bf16[2,768,768]{2,1,0:T(8,128)(2,1)} %param.8), kind=kOutput, calls=%fused_computation.51 | convolution fusion | flops 150994944 | bytes 2949120 | tf_op jit(solution)/shard_map/erd,edf->erf/dot_general | solution.py:51
  26.9 1.2 %convolution_convert_fusion.3 = bf16[2,64,768]{2,1,0:T(8,128)(2,1)} fusion(bf16[2,768,768]{2,1,0:T(8,128)(2,1)S(1)} %copy-done, f32[2,64,768]{2,1,0:T(8,128)S(1)} %fusion.34), kind=kOutput, calls=%fused_computation.6 | convolution fusion | flops 151584768 | bytes 2949120 | tf_op jit(solution)/shard_map/erf,efd->erd/dot_general | solution.py:53
  28.1 0.8 %fusion.1 = bf16[2,64,768]{2,1,0:T(8,128)(2,1)S(1)} fusion(bf16[2,64,768]{2,1,0:T(8,128)(2,1)S(1)} %reshape_squeeze.7, bf16[2,768,768]{2,1,0:T(8,128)(2,1)S(1)} %copy-done, f32[2,64,768]{2,1,0:T(8,128)S(1)} %fusion.34), kind=kOutput, calls=%fused_computation.7 | convolution fusion | flops 151977984 | bytes 3145728 | tf_op jit(solution)/shard_map/erd,efd->erf/dot_general | solution.py:54
  29.0 0.7 copy-done.3
  29.6 1.5 %convolution_convert_fusion.2 = bf16[2,64,768]{2,1,0:T(8,128)(2,1)} fusion(bf16[2,64,768]{2,1,0:T(8,128)(2,1)S(1)} %fusion.1, bf16[2,768,768]{2,1,0:T(8,128)(2,1)S(1)} %copy-done.1), kind=kOutput, calls=%fused_computation.5 | convolution fusion | flops 151093248 | bytes 2752512 | tf_op jit(solution)/shard_map/erf,edf->erd/dot_general | solution.py:56
  31.1 1.7 %stack.22 = bf16[1,2,32,1,2,768]{5,4,2,1,3,0:T(2,128)(2,1)} reshape(bf16[2,64,768]{2,1,0:T(8,128)(2,1)} %convolution_convert_fusion.2) | data formatting | bytes 393216 | tf_op jit(solution)/shard_map/stack | solution.py:57
  32.9 1.6 %copy.36 = bf16[1,2,32,1,2,768]{5,2,4,1,0,3:T(8,128)(2,1)} copy(bf16[1,2,32,1,2,768]{5,4,2,1,3,0:T(2,128)(2,1)} %stack.22) | data formatting | bytes 393216 | tf_op jit(solution)/shard_map/stack | solution.py:57
  34.5 1.7 %stack.21 = bf16[1,2,32,1,2,768]{5,4,2,1,3,0:T(2,128)(2,1)} reshape(bf16[2,64,768]{2,1,0:T(8,128)(2,1)} %convolution_convert_fusion.3) | data formatting | bytes 393216 | tf_op jit(solution)/shard_map/stack | solution.py:57
  36.2 0.9 %copy.35 = bf16[1,2,32,1,2,768]{5,2,4,1,0,3:T(8,128)(2,1)S(1)} copy(bf16[1,2,32,1,2,768]{5,4,2,1,3,0:T(2,128)(2,1)} %stack.21) | data formatting | bytes 393216 | tf_op jit(solution)/shard_map/stack | solution.py:57
  37.1 1.0 %pad_maximum_fusion = bf16[2,2,32,1,2,768]{5,2,4,1,0,3:T(8,128)(2,1)S(1)} fusion(bf16[1,2,32,1,2,768]{5,2,4,1,0,3:T(8,128)(2,1)} %copy.36, bf16[1,2,32,1,2,768]{5,2,4,1,0,3:T(8,128)(2,1)S(1)} %copy.35), kind=kLoop, calls=%fused_computation.16 | loop fusion | flops 196608 | bytes 786432 | tf_op jit(solution)/shard_map/stack | solution.py:57
  38.1 1.0 %copy.37 = bf16[32,8,768]{2,1,0:T(8,128)(2,1)} copy(bf16[32,8,768]{2,0,1:T(8,128)(2,1)S(1)} %bitcast.85) | data formatting | bytes 786432 | tf_op jit(solution)/shard_map/reshape | solution.py:60
  39.1 4.0 %all-to-all-start.1 = ((bf16[32,8,768]{2,1,0:T(8,128)(2,1)}), bf16[32,8,768]{2,1,0:T(8,128)(2,1)}, u32[]{:S(2)}, u32[]{:S(2)}) async-start(bf16[32,8,768]{2,1,0:T(8,128)(2,1)} %copy.37), calls=%async_computation.1 | async-start | bytes 786432 | tf_op jit(solution)/shard_map/all_to_all | solution.py:23
  43.0 0.9 %copy.47 = bf16[768,196]{1,0:T(8,128)(2,1)} copy(bf16[768,196]{0,1:T(8,128)(2,1)S(1)} %bitcast.83) | data formatting | bytes 602112 | tf_op jit(solution)/shard_map/btc,btd->cd/dot_general | solution.py:76
  44.0 3.2 %convolution_convert_fusion.1 = bf16[2,768,768]{2,1,0:T(8,128)(2,1)} fusion(bf16[2,64,768]{2,1,0:T(8,128)(2,1)S(1)} %reshape_squeeze.6, bf16[2,64,768]{2,1,0:T(8,128)(2,1)} %copy-done.3), kind=kOutput, calls=%fused_computation.1 | convolution fusion | flops 152174592 | bytes 2752512 | tf_op jit(solution)/shard_map/erd,erf->edf/dot_general | solution.py:62
  47.1 2.2 %convolution_convert_fusion = bf16[2,768,768]{2,1,0:T(8,128)(2,1)} fusion(bf16[2,64,768]{2,1,0:T(8,128)(2,1)S(1)} %reshape_squeeze.7, f32[2,64,768]{2,1,0:T(8,128)S(1)} %fusion.34), kind=kOutput, calls=%fused_computation | convolution fusion | flops 152666112 | bytes 2949120 | tf_op jit(solution)/shard_map/erf,erd->efd/dot_general | solution.py:61
  49.3 5.5 %all-to-all-done.1 = bf16[32,8,768]{2,1,0:T(8,128)(2,1)} async-done(((bf16[32,8,768]{2,1,0:T(8,128)(2,1)}), bf16[32,8,768]{2,1,0:T(8,128)(2,1)}, u32[]{:S(2)}, u32[]{:S(2)}) %all-to-all-start.1) | async-done | bytes 393248 | tf_op jit(solution)/shard_map/all_to_all | solution.py:23
  54.9 1.1 %reshape.143 = bf16[8,4,2,4,768]{4,3,2,1,0:T(4,128)(2,1)S(1)} reshape(bf16[32,8,768]{2,1,0:T(8,128)(2,1)} %all-to-all-done.1) | data formatting | bytes 786432 | tf_op jit(solution)/shard_map/reshape | solution.py:63
  56.0 0.9 %reduce_sum.61 = bf16[8,2,4,768]{3,2,1,0:T(4,128)(2,1)} reduce(bf16[8,4,2,4,768]{4,3,2,1,0:T(4,128)(2,1)S(1)} %reshape.143, bf16[]{:T(256)} %constant.7.clone.1), dimensions={1}, to_apply=%region_4.0 | reduce | flops 147456 | bytes 491522 | tf_op jit(solution)/shard_map/reduce_sum | solution.py:64
  56.8 0.9 %copy.52 = bf16[8,2,4,768]{3,0,2,1:T(8,128)(2,1)S(1)} copy(bf16[8,2,4,768]{3,2,1,0:T(4,128)(2,1)} %reduce_sum.61) | data formatting | bytes 196608
  59.0 0.8 %copy.40 = bf16[1,1,8,4,768]{4,3,2,1,0:T(4,128)(2,1)S(1)} copy(bf16[1,1,8,4,768]{4,2,3,0,1:T(8,128)(2,1)} %get-tuple-element.12) | data formatting | bytes 98304 | tf_op jit(solution)/shard_map/slice | solution.py:66
  59.8 0.6 reshape.145
  60.5 1.3 %fusion.12 = (f32[196]{0:T(256)S(1)}, f32[32]{0:T(128)S(1)}, f32[32,196]{1,0:T(8,128)S(1)}) fusion(f32[196]{0:T(256)} %copy-done.6, f32[196,32]{0,1:T(8,128)S(1)} %get-tuple-element.14, f32[196]{0:T(256)S(1)} %get-tuple-element.9, f32[32,196]{1,0:T(8,128)S(1)} %fusion.35, f32[32]{0:T(128)} %copy-done.7, f32[32]{0:T(128)} %copy-done.5, ...), kind=kOutput, calls=%fused_computation.33 | convolution fusion | flops 9683740 | bytes 428208 | tf_op jit(solution)/shard_map/btd,bcd->btc/dot_general | solution.py:67
  62.4 0.8 %fusion.7 = bf16[32,196]{1,0:T(8,128)(2,1)S(1)} fusion(f32[32,196]{1,0:T(8,128)S(1)} %fusion.35, f32[32,196]{1,0:T(8,128)S(1)} %get-tuple-element.15, f32[32]{0:T(128)S(1)} %get-tuple-element.5, f32[196]{0:T(256)S(1)} %get-tuple-element.4, f32[196]{0:T(256)} %copy-done.6, f32[196,32]{0,1:T(8,128)S(1)} %get-tuple-element.14, f32[196]{0:T(256)S(1)} %get-tuple-element.9, ...), kind=kLoop, calls=%fused_computation.23 | loop fusion | flops 62720 | bytes 90544 | tf_op jit(solution)/shard_map/convert_element_type | solution.py:71
  63.4 0.8 copy.43
  64.1 3.9 %all-to-all-start.2 = ((f32[32,4,192]{2,1,0:T(4,128)}), f32[32,4,192]{2,1,0:T(4,128)S(1)}, u32[]{:S(2)}, u32[]{:S(2)}) async-start(f32[32,4,192]{2,1,0:T(4,128)} %bitcast.19), calls=%async_computation.2 | async-start | bytes 262144 | tf_op jit(solution)/shard_map/all_to_all | solution.py:23
  68.0 1.9 %fusion = bf16[196,768]{1,0:T(8,128)(2,1)} fusion(f32[196,768]{1,0:T(8,128)S(1)} %fusion.23, bf16[768,32]{0,1:T(8,128)(2,1)} %param.7, f32[32,196]{1,0:T(8,128)S(1)} %fusion.35, f32[32,196]{1,0:T(8,128)S(1)} %get-tuple-element.15, f32[32]{0:T(128)} %copy-done.9, f32[196]{0:T(256)} %copy-done.8, f32[196,32]{0,1:T(8,128)S(1)} %get-tuple-element.14, ...), kind=kOutput, calls=%fused_computation.3 | convolution fusion | flops 9997568 | bytes 1030320 | tf_op jit(solution)/shard_map/btc,dc->btd/dot_general | solution.py:74
  69.9 6.5 %all-to-all-done.2 = f32[32,4,192]{2,1,0:T(4,128)S(1)} async-done(((f32[32,4,192]{2,1,0:T(4,128)}), f32[32,4,192]{2,1,0:T(4,128)S(1)}, u32[]{:S(2)}, u32[]{:S(2)}) %all-to-all-start.2) | async-done | bytes 98336 | tf_op jit(solution)/shard_map/all_to_all | solution.py:23
  76.4 0.6 reduce_sum.65
  (39 shorter events, 3.2 us)
Async XLA Ops:
  0.6 26.3 %copy-start = (bf16[2,768,768]{2,1,0:T(8,128)(2,1)S(1)}, bf16[2,768,768]{2,1,0:T(8,128)(2,1)}, u32[]{:S(2)}) copy-start(bf16[2,768,768]{2,1,0:T(8,128)(2,1)} %param.9) | copy-start | bytes 7077892
  2.1 56.5 %copy-start.5 = (f32[32]{0:T(128)}, f32[32]{0:T(128)S(1)}, u32[]{:S(2)}) copy-start(f32[32]{0:T(128)S(1)} %get-tuple-element.8) | copy-start | bytes 388
  2.3 21.8 %copy-start.6 = (f32[196]{0:T(256)}, f32[196]{0:T(256)S(1)}, u32[]{:S(2)}) copy-start(f32[196]{0:T(256)S(1)} %get-tuple-element.7) | copy-start | bytes 2356
  2.3 56.3 %copy-start.7 = (f32[32]{0:T(128)}, f32[32]{0:T(128)S(1)}, u32[]{:S(2)}) copy-start(f32[32]{0:T(128)S(1)} %get-tuple-element.6) | copy-start | bytes 388
  26.9 2.7 %copy-start.1 = (bf16[2,768,768]{2,1,0:T(8,128)(2,1)S(1)}, bf16[2,768,768]{2,1,0:T(8,128)(2,1)}, u32[]{:S(2)}) copy-start(bf16[2,768,768]{2,1,0:T(8,128)(2,1)} %param.8) | copy-start | bytes 7077892
  28.9 0.7 copy-start.3
  31.1 11.9 %copy-start.2 = (bf16[196,768]{1,0:T(8,128)(2,1)S(1)}, bf16[196,768]{1,0:T(8,128)(2,1)}, u32[]{:S(2)}) copy-start(bf16[196,768]{1,0:T(8,128)(2,1)} %param.5) | copy-start | bytes 903172
  39.1 15.8 %all-to-all-start.1 = ((bf16[32,8,768]{2,1,0:T(8,128)(2,1)}), bf16[32,8,768]{2,1,0:T(8,128)(2,1)}, u32[]{:S(2)}, u32[]{:S(2)}) async-start(bf16[32,8,768]{2,1,0:T(8,128)(2,1)} %copy.37), calls=%async_computation.1 | async-start | bytes 786432 | tf_op jit(solution)/shard_map/all_to_all | solution.py:23
  49.3 13.8 %copy-start.4 = (bf16[768,196]{1,0:T(8,128)(2,1)S(1)}, bf16[768,196]{1,0:T(8,128)(2,1)}, u32[]{:S(2)}) copy-start(bf16[768,196]{1,0:T(8,128)(2,1)} %copy.47) | copy-start | bytes 903172
  61.8 0.6 copy-start.8
  61.8 0.6 copy-start.9
  64.1 12.3 %all-to-all-start.2 = ((f32[32,4,192]{2,1,0:T(4,128)}), f32[32,4,192]{2,1,0:T(4,128)S(1)}, u32[]{:S(2)}, u32[]{:S(2)}) async-start(f32[32,4,192]{2,1,0:T(4,128)} %bitcast.19), calls=%async_computation.2 | async-start | bytes 262144 | tf_op jit(solution)/shard_map/all_to_all | solution.py:23

commit v2 on v1

v2 whole, which is shorter than its diff:
```python
import functools

import jax
import jax.numpy as jnp
from jax import lax
from jax.experimental import pallas as pl
from jax.experimental.pallas import tpu as pltpu
from jax.sharding import PartitionSpec as P

SLOTS = 2
TOK = 196
BOTH = ("expert", "hidden")
F32, BF16 = jnp.float32, jnp.bfloat16
NN = (((1,), (0,)), ((), ()))
NT = (((1,), (1,)), ((), ()))
TN = (((0,), (0,)), ((), ()))


def dot(left, right, dims=NN):
    return lax.dot_general(left, right, dims, preferred_element_type=F32)


def reorder(shape, old_axes, rows):
    out_row = lax.broadcasted_iota(jnp.int32, (rows, 1), 0)
    strides = [1] * len(shape)
    for axis in reversed(range(len(shape) - 1)):
        strides[axis] = strides[axis + 1] * shape[axis + 1]
    source = jnp.zeros_like(out_row)
    rest = out_row
    for axis in reversed(old_axes):
        source = source + lax.rem(rest, shape[axis]) * strides[axis]
        rest = lax.div(rest, shape[axis])
    columns = lax.broadcasted_iota(jnp.int32, (rows, rows), 1)
    return jnp.where(columns == source, 1.0, 0.0).astype(BF16)


def softmaxes(logits):
    by_token = jnp.exp(logits - jnp.max(logits, axis=1, keepdims=True))
    dispatch = by_token / jnp.sum(by_token, axis=1, keepdims=True)
    by_slot = jnp.exp(logits - jnp.max(logits, axis=0, keepdims=True))
    combine = by_slot / jnp.sum(by_slot, axis=0, keepdims=True)
    return dispatch, combine


def slots_kernel(dims, tokens, out_grad, router, logits_out, sent):
    n_expert, n_hidden, local_slots = dims
    images, _, width = tokens.shape
    slots = n_expert * local_slots
    order = reorder((2, n_expert, local_slots), (1, 0, 2), 2 * slots)
    for image in range(images):
        logits = dot(router[...], tokens[image], NT)
        logits_out[image] = logits
        dispatch, combine = softmaxes(logits)
        slot_in = dot(dispatch.astype(BF16), tokens[image]).astype(BF16)
        slot_grad = dot(combine.astype(BF16), out_grad[image]).astype(BF16)
        both = dot(order, jnp.concatenate([slot_in, slot_grad], axis=0)).astype(BF16)
        both = both.reshape(n_expert, 2 * local_slots, width)
        for copy in range(n_hidden):
            sent[:, copy, image] = both


def experts_kernel(dims, received, weight_in, weight_out, parts, rows_out, act_out, d_pre_out):
    images, local_experts, chunk = dims
    devices, per_source, width = received.shape
    shape = (chunk, images, 2, local_experts, SLOTS)
    size = chunk * per_source
    part = size // (2 * local_experts)
    to_expert = (2, 3, 0, 1, 4)
    order = reorder(shape, to_expert, size)
    moved = tuple(shape[axis] for axis in to_expert)
    back = reorder(moved, tuple(to_expert.index(axis) for axis in range(5)), size)
    for start in range(0, devices, chunk):
        block = received[start : start + chunk].reshape(size, width)
        rows = dot(order, block).astype(BF16)
        base = start // chunk * part
        forwards, backwards = [], []
        for expert in range(local_experts):
            slot_in = rows[expert * part : (expert + 1) * part]
            slot_grad = rows[(local_experts + expert) * part : (local_experts + expert + 1) * part]
            rows_out[0, expert, base : base + part] = slot_in
            rows_out[1, expert, base : base + part] = slot_grad
            pre = dot(slot_in, weight_in[expert])
            d_act = dot(slot_grad, weight_out[expert], NT)
            half = 0.5 * (1.0 + lax.erf(pre * 0.7071067811865476))
            act = (pre * half).astype(BF16)
            slope = half + pre * jnp.exp(-0.5 * pre * pre) * 0.3989422804014327
            d_pre = (d_act * slope).astype(BF16)
            act_out[expert, base : base + part] = act
            d_pre_out[expert, base : base + part] = d_pre
            forwards.append(dot(act, weight_out[expert]).astype(BF16))
            backwards.append(dot(d_pre, weight_in[expert], NT).astype(BF16))
        results = dot(back, jnp.concatenate(forwards + backwards, axis=0)).astype(BF16)
        parts[start : start + chunk] = results.reshape(chunk, per_source, width)


def weights_kernel(rows, act, d_pre, grad_in, grad_out):
    grad_in[0] = dot(rows[0, 0], d_pre[0], TN).astype(BF16)
    grad_out[0] = dot(act[0], rows[1, 0], TN).astype(BF16)


def images_kernel(dims, logits_in, tokens, out_grad, router, parts, token_grad, terms):
    n_expert, n_hidden, local_slots = dims
    images, _, width = tokens.shape
    slots = n_expert * local_slots
    order = reorder((n_expert, 2, local_slots), (1, 0, 2), 2 * slots)
    total = None
    for image in range(images):
        dispatch, combine = softmaxes(logits_in[image])
        summed = parts[:, 0, image].astype(F32)
        for part in range(1, n_hidden):
            summed = summed + parts[:, part, image].astype(F32)
        summed = summed.reshape(2 * slots, width).astype(BF16)
        both = dot(order, summed).astype(BF16)
        slot_out, slot_in_grad = both[:slots], both[slots:]
        d_combine = dot(slot_out, out_grad[image], NT)
        d_dispatch = dot(slot_in_grad, tokens[image], NT)
        from_combine = combine * (d_combine - jnp.sum(combine * d_combine, axis=0, keepdims=True))
        from_dispatch = dispatch * (
            d_dispatch - jnp.sum(dispatch * d_dispatch, axis=1, keepdims=True)
        )
        d_logits = (from_combine + from_dispatch).astype(BF16)
        term = dot(d_logits, tokens[image])
        total = term if total is None else total + term
        left = jnp.concatenate([dispatch.astype(BF16), d_logits], axis=0)
        right = jnp.concatenate([slot_in_grad, router[...]], axis=0)
        token_grad[image] = dot(left, right, TN).astype(BF16)
    block = width // n_hidden
    for part in range(n_hidden):
        columns = total[:, part * block : (part + 1) * block]
        terms[:, part] = columns.reshape(n_expert, local_slots, block)


def exchange(blocks):
    return lax.all_to_all(blocks, BOTH, split_axis=0, concat_axis=0, tiled=True)


def call(kernel, outs, args, flops, **more):
    moved = sum(x.size * x.dtype.itemsize for x in list(outs) + list(args))
    return pl.pallas_call(
        kernel,
        out_shape=outs,
        cost_estimate=pl.CostEstimate(flops=flops, bytes_accessed=moved, transcendentals=0),
        compiler_params=pltpu.CompilerParams(vmem_limit_bytes=40 * 2**20),
        **more,
    )(*args)


def per_device(n_expert, n_hidden, tokens, out_grad, slot_router, weight_in, weight_out):
    width = tokens.shape[1]
    images = tokens.shape[0] // TOK
    local_experts, _, hidden = weight_in.shape
    local_slots = local_experts * SLOTS
    slots = n_expert * local_slots
    devices = n_expert * n_hidden
    per_source = 2 * images * local_slots
    rows = devices * images * SLOTS
    shape = jax.ShapeDtypeStruct
    inputs = tokens.reshape(images, TOK, width)
    out_grads = out_grad.reshape(images, TOK, width)
    router = slot_router.T
    dims = (n_expert, n_hidden, local_slots)

    logits, sent = call(
        functools.partial(slots_kernel, dims),
        (
            shape((images, slots, TOK), F32),
            shape((n_expert, n_hidden, images, 2 * local_slots, width), BF16),
        ),
        (inputs, out_grads, router),
        6 * images * slots * TOK * width,
    )
    received = exchange(sent.reshape(devices, per_source, width))
    chunk = max(c for c in range(1, devices + 1) if devices % c == 0 and c * per_source <= 256)
    parts, slot_rows, act, d_pre = call(
        functools.partial(experts_kernel, (images, local_experts, chunk)),
        (
            shape((devices, per_source, width), BF16),
            shape((2, local_experts, rows, width), BF16),
            shape((local_experts, rows, hidden), BF16),
            shape((local_experts, rows, hidden), BF16),
        ),
        (received, weight_in, weight_out),
        8 * local_experts * rows * width * hidden,
    )
    back = exchange(parts)
    grad_in, grad_out = call(
        weights_kernel,
        (
            shape((local_experts, width, hidden), BF16),
            shape((local_experts, hidden, width), BF16),
        ),
        (slot_rows, act, d_pre),
        4 * local_experts * rows * width * hidden,
        grid=(local_experts,),
        in_specs=[
            pl.BlockSpec((2, 1, rows, width), lambda e: (0, e, 0, 0)),
            pl.BlockSpec((1, rows, hidden), lambda e: (e, 0, 0)),
            pl.BlockSpec((1, rows, hidden), lambda e: (e, 0, 0)),
        ],
        out_specs=[
            pl.BlockSpec((1, width, hidden), lambda e: (e, 0, 0)),
            pl.BlockSpec((1, hidden, width), lambda e: (e, 0, 0)),
        ],
    )
    token_grad, terms = call(
        functools.partial(images_kernel, dims),
        (
            shape((images, TOK, width), BF16),
            shape((n_expert, n_hidden, local_slots, width // n_hidden), F32),
        ),
        (
            logits,
            inputs,
            out_grads,
            router,
            back.reshape(n_expert, n_hidden, images, 2 * local_slots, width),
        ),
        10 * images * slots * TOK * width,
    )
    router_parts = exchange(terms.reshape(devices, local_slots, width // n_hidden))
    router_grad = jnp.sum(router_parts, axis=0).T
    return token_grad.reshape(images * TOK, width), router_grad, grad_in, grad_out


def solution(mesh):
    return jax.shard_map(
        functools.partial(per_device, mesh.shape["expert"], mesh.shape["hidden"]),
        mesh=mesh,
        in_specs=(
            P(BOTH, None),
            P(BOTH, None),
            P(),
            P("expert", None, "hidden"),
            P("expert", "hidden", None),
        ),
        out_specs=(
            P(BOTH, None),
            P("hidden", "expert"),
            P("expert", None, "hidden"),
            P("expert", "hidden", None),
        ),
        check_vma=False,
    )
```

time: 77.8 us -> 59.4 us (0.76)
  matrix products: 18.9 us -> 0 us
  blocking collectives: 18.9 us -> 34.4 us
  local copies, waits for them, and re-layouts: 15 us -> 6.07 us
  Pallas kernels: 0 us -> 7.82 us
  waiting for transfers between devices: 12 us -> 5.53 us
  starting transfers between devices: 7.83 us -> 3.86 us
  other arithmetic: 3.51 us -> 0.64 us
    dot_general x14 -> x0, matrix products: 18.9 us -> none  [the longest x1 3.16 us: per_device(): jnp.einsum('erd,erf->edf', slot_inputs, d_pre, preferred_element_type=f32)]
    all_to_all x1 -> x2, blocking collectives: 18.9 us -> 34.4 us  [exchange(): return lax.all_to_all(blocks, BOTH, split_axis=0, concat_axis=0, tiled=True)]
    pallas_call x0 -> x4, Pallas kernels: none -> 7.82 us  [call(): pl.pallas_call(kernel, out_shape=outs, cost_estimate=pl.CostEstimate(flop...]
    another operation x10 -> x0, local copies, waits for them, and re-layouts: 6.85 us -> none  [the longest x4 5.97 us: per_device(): partials = jnp.stack([forward.astype(bf16), backward.astype(bf16)])]
    all_to_all x2 -> x1, waiting for transfers between devices: 12 us -> 5.53 us  [exchange(): return lax.all_to_all(blocks, BOTH, split_axis=0, concat_axis=0, tiled=True)]
    all_to_all x2 -> x1, starting transfers between devices: 7.83 us -> 3.86 us  [exchange(): return lax.all_to_all(blocks, BOTH, split_axis=0, concat_axis=0, tiled=True)]
    unnamed x21 -> x16, local copies, waits for them, and re-layouts: 2.19 us -> 6.07 us
    reshape x3 -> x0, local copies, waits for them, and re-layouts: 2.15 us -> none  [the longest x1 1.09 us: per_device(): back = back.reshape(n_expert, n_hidden, 2, images, local_slots, width)]
  transfers between devices with their start and end apart: 2 -> 1, of which waited for: 2 -> 1; matrix products, arithmetic and copies ran while one was open for 11% -> 0% of each run, Pallas kernels for 0% -> 5%
where the time goes in v2:
time: 59.4 us; the launch traced here: 59 us
  blocking collectives  34.4 us (58%)
  Pallas kernels  7.82 us (13%)
  local copies, waits for them, and re-layouts  6.07 us (10%)
  waiting for transfers between devices  5.53 us (9%)
  starting transfers between devices  3.86 us (6%)
  between operations  0.67 us (1%)
  other arithmetic  0.64 us (1%)
    all_to_all x2, blocking collectives, exchange(): return lax.all_to_all(blocks, BOTH, split_axis=0, concat_axis=0, tiled=True)  34.4 us
    pallas_call x4, Pallas kernels, call(): pl.pallas_call(kernel, out_shape=outs, cost_estimate=pl.CostEstimate(flop...  7.82 us
    unnamed x16, local copies, waits for them, and re-layouts  6.07 us
    all_to_all x1, waiting for transfers between devices, exchange(): return lax.all_to_all(blocks, BOTH, split_axis=0, concat_axis=0, tiled=True)  5.53 us
    all_to_all x1, starting transfers between devices, exchange(): return lax.all_to_all(blocks, BOTH, split_axis=0, concat_axis=0, tiled=True)  3.86 us
  transfers between devices with their start and end apart: 1, of which 1 were waited for; matrix products, arithmetic and copies ran while one was open for 0% of the time, Pallas kernels for 5%

profile of v2, /device:TPU:0, one launch (start us, length us, event | category | flops | bytes accessed | tf_op | source)
XLA Modules:
  0.0 59.0 jit_solution(1953548920208575380)
XLA Ops:
  0.6 0.0 copy-start.2
  0.6 1.0 %copy-done.2 = bf16[196,768]{1,0:T(8,128)(2,1)S(1)} copy-done((bf16[196,768]{1,0:T(8,128)(2,1)S(1)}, bf16[196,768]{1,0:T(8,128)(2,1)}, u32[]{:S(2)}) %copy-start.2) | copy-done | bytes 301080
  1.6 0.0 copy-start.4
  1.6 1.0 %copy-done.4 = bf16[196,768]{1,0:T(8,128)(2,1)S(1)} copy-done((bf16[196,768]{1,0:T(8,128)(2,1)S(1)}, bf16[196,768]{1,0:T(8,128)(2,1)}, u32[]{:S(2)}) %copy-start.4) | copy-done | bytes 301080
  2.6 0.0 copy-start.6
  2.6 0.8 %copy-done.6 = bf16[768,32]{0,1:T(8,128)(2,1)S(1)} copy-done((bf16[768,32]{0,1:T(8,128)(2,1)S(1)}, bf16[768,32]{0,1:T(8,128)(2,1)}, u32[]{:S(2)}) %copy-start.6) | copy-done | bytes 49176
  3.4 0.8 %shard_map.84 = (f32[1,32,196]{2,1,0:T(8,128)S(1)}, bf16[8,4,1,8,768]{4,3,2,1,0:T(8,128)(2,1)S(1)}) custom-call(bf16[1,196,768]{2,1,0:T(8,128)(2,1)S(1)} %bitcast.9, bf16[1,196,768]{2,1,0:T(8,128)(2,1)S(1)} %bitcast.11, bf16[32,768]{1,0:T(8,128)(2,1)S(1)} %bitcast.14), custom_call_target="tpu_custom_call" | custom-call | flops 28901376 | bytes 1069568 | tf_op jit(solution)/shard_map/pallas_call | solution.py:139
  4.2 18.9 %all_to_all.15.received = bf16[32,8,768]{2,1,0:T(8,128)(2,1)S(1)} all-to-all(bf16[32,8,768]{2,1,0:T(8,128)(2,1)S(1)} %bitcast.13), channel_id=1, replica_groups=mesh['expert'=8,'hidden'=4] {'expert','hidden'}, dimensions={0} | all-to-all | bytes 786432 | tf_op jit(solution)/shard_map/all_to_all | solution.py:134
  23.1 0.0 copy-start
  23.1 1.7 %copy-done = bf16[2,768,768]{2,1,0:T(8,128)(2,1)S(1)} copy-done((bf16[2,768,768]{2,1,0:T(8,128)(2,1)S(1)}, bf16[2,768,768]{2,1,0:T(8,128)(2,1)}, u32[]{:S(2)}) %copy-start) | copy-done | bytes 2359320
  24.8 0.0 copy-start.1
  24.8 1.7 %copy-done.1 = bf16[2,768,768]{2,1,0:T(8,128)(2,1)S(1)} copy-done((bf16[2,768,768]{2,1,0:T(8,128)(2,1)S(1)}, bf16[2,768,768]{2,1,0:T(8,128)(2,1)}, u32[]{:S(2)}) %copy-start.1) | copy-done | bytes 2359320
  26.5 0.0 copy-start.3
  26.5 0.0 copy-start.5
  26.5 0.0 copy-start.7
  26.5 2.6 %shard_map.85 = (bf16[32,8,768]{2,1,0:T(8,128)(2,1)S(1)}, bf16[2,2,64,768]{3,2,1,0:T(8,128)(2,1)S(1)}, bf16[2,64,768]{2,1,0:T(8,128)(2,1)S(1)}, bf16[2,64,768]{2,1,0:T(8,128)(2,1)S(1)}) custom-call(bf16[32,8,768]{2,1,0:T(8,128)(2,1)S(1)} %all_to_all.15.received, bf16[2,768,768]{2,1,0:T(8,128)(2,1)S(1)} %copy-done, bf16[2,768,768]{2,1,0:T(8,128)(2,1)S(1)} %copy-done.1), custom_call_target="tpu_custom_call" | custom-call | flops 603979776 | bytes 6291456 | tf_op jit(solution)/shard_map/pallas_call | solution.py:139
  29.1 15.5 %all_to_all.16 = bf16[32,8,768]{2,1,0:T(8,128)(2,1)S(1)} all-to-all(bf16[32,8,768]{2,1,0:T(8,128)(2,1)S(1)} %get-tuple-element.16), channel_id=1, replica_groups=mesh['expert'=8,'hidden'=4] {'expert','hidden'}, dimensions={0} | all-to-all | bytes 786432 | tf_op jit(solution)/shard_map/all_to_all | solution.py:134
  44.6 0.0 copy-done.3
  44.6 0.0 copy-done.5
  44.6 0.0 copy-done.7
  44.6 1.5 %shard_map.86 = (bf16[1,196,768]{2,1,0:T(8,128)(2,1)}, f32[8,4,4,192]{3,2,1,0:T(4,128)}) custom-call(f32[1,32,196]{2,1,0:T(8,128)S(1)} %get-tuple-element.14.logits_in, bf16[1,196,768]{2,1,0:T(8,128)(2,1)S(1)} %bitcast.10, bf16[1,196,768]{2,1,0:T(8,128)(2,1)S(1)} %bitcast.12, bf16[32,768]{1,0:T(8,128)(2,1)S(1)} %bitcast.15, ...), custom_call_target="tpu_custom_call" | custom-call | flops 48168960 | bytes 1468928 | tf_op jit(solution)/shard_map/pallas_call | solution.py:139
  46.1 3.9 %all-to-all-start.2 = ((f32[32,4,192]{2,1,0:T(4,128)}), f32[32,4,192]{2,1,0:T(4,128)S(1)}, u32[]{:S(2)}, u32[]{:S(2)}) async-start(f32[32,4,192]{2,1,0:T(4,128)} %bitcast.6), calls=%async_computation.2 | async-start | bytes 262144 | tf_op jit(solution)/shard_map/all_to_all | solution.py:134
  50.0 2.9 %shard_map.87 = (bf16[2,768,768]{2,1,0:T(8,128)(2,1)}, bf16[2,768,768]{2,1,0:T(8,128)(2,1)}) custom-call(bf16[2,2,64,768]{3,2,1,0:T(8,128)(2,1)S(1)} %get-tuple-element.19.rows, bf16[2,64,768]{2,1,0:T(8,128)(2,1)S(1)} %get-tuple-element.20.act, bf16[2,64,768]{2,1,0:T(8,128)(2,1)S(1)} %get-tuple-element.21.d_pre), custom_call_target="tpu_custom_call" | custom-call | flops 301989888 | bytes 5505024 | tf_op jit(solution)/shard_map/pallas_call | solution.py:139
  52.8 5.5 %all-to-all-done.2 = f32[32,4,192]{2,1,0:T(4,128)S(1)} async-done(((f32[32,4,192]{2,1,0:T(4,128)}), f32[32,4,192]{2,1,0:T(4,128)S(1)}, u32[]{:S(2)}, u32[]{:S(2)}) %all-to-all-start.2) | async-done | bytes 98336 | tf_op jit(solution)/shard_map/all_to_all | solution.py:134
  58.4 0.6 %reduce_sum.9 = f32[4,192]{1,0:T(4,128)} reduce(f32[32,4,192]{2,1,0:T(4,128)S(1)} %all-to-all-done.2, f32[]{:T(128)} %constant.0.clone.1), dimensions={0}, to_apply=%region_0.0 | reduce | flops 23808 | bytes 101380 | tf_op jit(solution)/shard_map/reduce_sum | solution.py:221
Async XLA Ops:
  0.6 1.0 %copy-start.2 = (bf16[196,768]{1,0:T(8,128)(2,1)S(1)}, bf16[196,768]{1,0:T(8,128)(2,1)}, u32[]{:S(2)}) copy-start(bf16[196,768]{1,0:T(8,128)(2,1)} %param.5) | copy-start | bytes 903172
  1.6 1.0 %copy-start.4 = (bf16[196,768]{1,0:T(8,128)(2,1)S(1)}, bf16[196,768]{1,0:T(8,128)(2,1)}, u32[]{:S(2)}) copy-start(bf16[196,768]{1,0:T(8,128)(2,1)} %param.6) | copy-start | bytes 903172
  2.6 0.8 %copy-start.6 = (bf16[768,32]{0,1:T(8,128)(2,1)S(1)}, bf16[768,32]{0,1:T(8,128)(2,1)}, u32[]{:S(2)}) copy-start(bf16[768,32]{0,1:T(8,128)(2,1)} %param.7) | copy-start | bytes 147460
  23.1 1.7 %copy-start = (bf16[2,768,768]{2,1,0:T(8,128)(2,1)S(1)}, bf16[2,768,768]{2,1,0:T(8,128)(2,1)}, u32[]{:S(2)}) copy-start(bf16[2,768,768]{2,1,0:T(8,128)(2,1)} %weight_in.1) | copy-start | bytes 7077892
  24.8 1.7 %copy-start.1 = (bf16[2,768,768]{2,1,0:T(8,128)(2,1)S(1)}, bf16[2,768,768]{2,1,0:T(8,128)(2,1)}, u32[]{:S(2)}) copy-start(bf16[2,768,768]{2,1,0:T(8,128)(2,1)} %weight_out.1) | copy-start | bytes 7077892
  26.5 18.1 %copy-start.3 = (bf16[196,768]{1,0:T(8,128)(2,1)S(1)}, bf16[196,768]{1,0:T(8,128)(2,1)}, u32[]{:S(2)}) copy-start(bf16[196,768]{1,0:T(8,128)(2,1)} %param.5) | copy-start | bytes 903172
  26.5 18.1 %copy-start.5 = (bf16[196,768]{1,0:T(8,128)(2,1)S(1)}, bf16[196,768]{1,0:T(8,128)(2,1)}, u32[]{:S(2)}) copy-start(bf16[196,768]{1,0:T(8,128)(2,1)} %param.6) | copy-start | bytes 903172
  26.5 18.2 %copy-start.7 = (bf16[768,32]{0,1:T(8,128)(2,1)S(1)}, bf16[768,32]{0,1:T(8,128)(2,1)}, u32[]{:S(2)}) copy-start(bf16[768,32]{0,1:T(8,128)(2,1)} %param.7) | copy-start | bytes 147460
  46.1 12.3 %all-to-all-start.2 = ((f32[32,4,192]{2,1,0:T(4,128)}), f32[32,4,192]{2,1,0:T(4,128)S(1)}, u32[]{:S(2)}, u32[]{:S(2)}) async-start(f32[32,4,192]{2,1,0:T(4,128)} %bitcast.6), calls=%async_computation.2 | async-start | bytes 262144 | tf_op jit(solution)/shard_map/all_to_all | solution.py:134

commit v3 on v2

--- a/solution.py
+++ b/solution.py
@@ -42,16 +42,29 @@
     return dispatch, combine
 
 
-def slots_kernel(dims, tokens, out_grad, router, logits_out, sent):
+def slots_kernel(dims, tokens_hbm, out_grad_hbm, router_hbm, logits_out, sent, *scratch):
+    tokens, out_grad, router, sems = scratch
     n_expert, n_hidden, local_slots = dims
     images, _, width = tokens.shape
     slots = n_expert * local_slots
+    copies = [
+        pltpu.make_async_copy(source, target, sems.at[i])
+        for i, (source, target) in enumerate(
+            ((router_hbm, router), (tokens_hbm, tokens), (out_grad_hbm, out_grad))
+        )
+    ]
+    for copy in copies:
+        copy.start()
     order = reorder((2, n_expert, local_slots), (1, 0, 2), 2 * slots)
+    copies[0].wait()
+    copies[1].wait()
     for image in range(images):
         logits = dot(router[...], tokens[image], NT)
         logits_out[image] = logits
         dispatch, combine = softmaxes(logits)
         slot_in = dot(dispatch.astype(BF16), tokens[image]).astype(BF16)
+        if image == 0:
+            copies[2].wait()
         slot_grad = dot(combine.astype(BF16), out_grad[image]).astype(BF16)
         both = dot(order, jnp.concatenate([slot_in, slot_grad], axis=0)).astype(BF16)
         both = both.reshape(n_expert, 2 * local_slots, width)
@@ -166,8 +179,15 @@
             shape((images, slots, TOK), F32),
             shape((n_expert, n_hidden, images, 2 * local_slots, width), BF16),
         ),
-        (inputs, out_grads, router),
-        6 * images * slots * TOK * width,
+        tuple(pltpu.with_memory_space_constraint(x, pltpu.HBM) for x in (inputs, out_grads, router)),
+        8 * local_experts * rows * width * hidden * n_expert,
+        in_specs=[pl.BlockSpec(memory_space=pltpu.HBM)] * 3,
+        scratch_shapes=[
+            pltpu.VMEM(inputs.shape, BF16),
+            pltpu.VMEM(out_grads.shape, BF16),
+            pltpu.VMEM(router.shape, BF16),
+            pltpu.SemaphoreType.DMA((3,)),
+        ],
     )
     received = exchange(sent.reshape(devices, per_source, width))
     chunk = max(c for c in range(1, devices + 1) if devices % c == 0 and c * per_source <= 256)

time: 59.4 us -> 54.5 us (0.918)
  local copies, waits for them, and re-layouts: 6.07 us -> 0.02 us
  Pallas kernels: 7.82 us -> 9.11 us
    unnamed x16 -> x10, local copies, waits for them, and re-layouts: 6.07 us -> 0.02 us
    pallas_call x4, Pallas kernels: 7.82 us -> 9.11 us  [call(): pl.pallas_call(kernel, out_shape=outs, cost_estimate=pl.CostEstimate(flop...]
where the time goes in v3:
time: 54.5 us; the launch traced here: 54.3 us
  blocking collectives  34.4 us (63%)
  Pallas kernels  9.11 us (17%)
  waiting for transfers between devices  5.53 us (10%)
  starting transfers between devices  3.86 us (7%)
  between operations  0.69 us (1%)
  other arithmetic  0.64 us (1%)
    all_to_all x2, blocking collectives, exchange(): return lax.all_to_all(blocks, BOTH, split_axis=0, concat_axis=0, tiled=True)  34.4 us
    pallas_call x4, Pallas kernels, call(): pl.pallas_call(kernel, out_shape=outs, cost_estimate=pl.CostEstimate(flop...  9.11 us
    all_to_all x1, waiting for transfers between devices, exchange(): return lax.all_to_all(blocks, BOTH, split_axis=0, concat_axis=0, tiled=True)  5.53 us
    all_to_all x1, starting transfers between devices, exchange(): return lax.all_to_all(blocks, BOTH, split_axis=0, concat_axis=0, tiled=True)  3.86 us
  transfers between devices with their start and end apart: 1, of which 1 were waited for; matrix products, arithmetic and copies ran while one was open for 0% of the time, Pallas kernels for 5%

profile of v3, /device:TPU:0, one launch (start us, length us, event | category | flops | bytes accessed | tf_op | source)
XLA Modules:
  0.0 54.3 jit_solution(12593572900920778289)
XLA Ops:
  0.6 0.0 copy-start
  0.6 0.0 copy-start.1
  0.7 2.1 %shard_map.84 = (f32[1,32,196]{2,1,0:T(8,128)S(1)}, bf16[8,4,1,8,768]{4,3,2,1,0:T(8,128)(2,1)S(1)}) custom-call(bf16[1,196,768]{2,1,0:T(8,128)(2,1)} %bitcast.10, bf16[1,196,768]{2,1,0:T(8,128)(2,1)} %bitcast.12, bf16[32,768]{1,0:T(8,128)(2,1)} %bitcast.14), custom_call_target="tpu_custom_call" | custom-call | flops 4831838208 | bytes 1069568 | tf_op jit(solution)/shard_map/pallas_call | solution.py:152
  2.8 18.9 %all_to_all.15.received = bf16[32,8,768]{2,1,0:T(8,128)(2,1)S(1)} all-to-all(bf16[32,8,768]{2,1,0:T(8,128)(2,1)S(1)} %bitcast.9), channel_id=1, replica_groups=mesh['expert'=8,'hidden'=4] {'expert','hidden'}, dimensions={0} | all-to-all | bytes 786432 | tf_op jit(solution)/shard_map/all_to_all | solution.py:147
  21.7 0.0 copy-done
  21.7 0.0 copy-done.1
  21.7 0.0 copy-start.2
  21.7 0.0 copy-start.3
  21.7 0.0 copy-start.4
  21.7 2.6 %shard_map.85 = (bf16[32,8,768]{2,1,0:T(8,128)(2,1)S(1)}, bf16[2,2,64,768]{3,2,1,0:T(8,128)(2,1)S(1)}, bf16[2,64,768]{2,1,0:T(8,128)(2,1)S(1)}, bf16[2,64,768]{2,1,0:T(8,128)(2,1)S(1)}) custom-call(bf16[32,8,768]{2,1,0:T(8,128)(2,1)S(1)} %all_to_all.15.received, bf16[2,768,768]{2,1,0:T(8,128)(2,1)S(1)} %copy-done, bf16[2,768,768]{2,1,0:T(8,128)(2,1)S(1)} %copy-done.1), custom_call_target="tpu_custom_call" | custom-call | flops 603979776 | bytes 6291456 | tf_op jit(solution)/shard_map/pallas_call | solution.py:152
  24.4 15.5 %all_to_all.16 = bf16[32,8,768]{2,1,0:T(8,128)(2,1)S(1)} all-to-all(bf16[32,8,768]{2,1,0:T(8,128)(2,1)S(1)} %get-tuple-element.16), channel_id=1, replica_groups=mesh['expert'=8,'hidden'=4] {'expert','hidden'}, dimensions={0} | all-to-all | bytes 786432 | tf_op jit(solution)/shard_map/all_to_all | solution.py:147
  39.9 0.0 copy-done.2
  39.9 0.0 copy-done.3
  39.9 0.0 copy-done.4
  39.9 1.5 %shard_map.86 = (bf16[1,196,768]{2,1,0:T(8,128)(2,1)}, f32[8,4,4,192]{3,2,1,0:T(4,128)}) custom-call(f32[1,32,196]{2,1,0:T(8,128)S(1)} %get-tuple-element.14.logits_in, bf16[1,196,768]{2,1,0:T(8,128)(2,1)S(1)} %bitcast.11, bf16[1,196,768]{2,1,0:T(8,128)(2,1)S(1)} %bitcast.13, bf16[32,768]{1,0:T(8,128)(2,1)S(1)} %bitcast.15, ...), custom_call_target="tpu_custom_call" | custom-call | flops 48168960 | bytes 1468928 | tf_op jit(solution)/shard_map/pallas_call | solution.py:152
  41.4 3.9 %all-to-all-start.2 = ((f32[32,4,192]{2,1,0:T(4,128)}), f32[32,4,192]{2,1,0:T(4,128)S(1)}, u32[]{:S(2)}, u32[]{:S(2)}) async-start(f32[32,4,192]{2,1,0:T(4,128)} %bitcast.6), calls=%async_computation.2 | async-start | bytes 262144 | tf_op jit(solution)/shard_map/all_to_all | solution.py:147
  45.2 2.9 %shard_map.87 = (bf16[2,768,768]{2,1,0:T(8,128)(2,1)}, bf16[2,768,768]{2,1,0:T(8,128)(2,1)}) custom-call(bf16[2,2,64,768]{3,2,1,0:T(8,128)(2,1)S(1)} %get-tuple-element.19.rows, bf16[2,64,768]{2,1,0:T(8,128)(2,1)S(1)} %get-tuple-element.20.act, bf16[2,64,768]{2,1,0:T(8,128)(2,1)S(1)} %get-tuple-element.21.d_pre), custom_call_target="tpu_custom_call" | custom-call | flops 301989888 | bytes 5505024 | tf_op jit(solution)/shard_map/pallas_call | solution.py:152
  48.1 5.5 %all-to-all-done.2 = f32[32,4,192]{2,1,0:T(4,128)S(1)} async-done(((f32[32,4,192]{2,1,0:T(4,128)}), f32[32,4,192]{2,1,0:T(4,128)S(1)}, u32[]{:S(2)}, u32[]{:S(2)}) %all-to-all-start.2) | async-done | bytes 98336 | tf_op jit(solution)/shard_map/all_to_all | solution.py:147
  53.6 0.6 %reduce_sum.9 = f32[4,192]{1,0:T(4,128)} reduce(f32[32,4,192]{2,1,0:T(4,128)S(1)} %all-to-all-done.2, f32[]{:T(128)} %constant.0.clone.1), dimensions={0}, to_apply=%region_0.0 | reduce | flops 23808 | bytes 101380 | tf_op jit(solution)/shard_map/reduce_sum | solution.py:241
Async XLA Ops:
  0.6 21.1 %copy-start = (bf16[2,768,768]{2,1,0:T(8,128)(2,1)S(1)}, bf16[2,768,768]{2,1,0:T(8,128)(2,1)}, u32[]{:S(2)}) copy-start(bf16[2,768,768]{2,1,0:T(8,128)(2,1)} %weight_in.1) | copy-start | bytes 7077892
  0.6 21.1 %copy-start.1 = (bf16[2,768,768]{2,1,0:T(8,128)(2,1)S(1)}, bf16[2,768,768]{2,1,0:T(8,128)(2,1)}, u32[]{:S(2)}) copy-start(bf16[2,768,768]{2,1,0:T(8,128)(2,1)} %weight_out.1) | copy-start | bytes 7077892
  21.7 18.2 %copy-start.2 = (bf16[196,768]{1,0:T(8,128)(2,1)S(1)}, bf16[196,768]{1,0:T(8,128)(2,1)}, u32[]{:S(2)}) copy-start(bf16[196,768]{1,0:T(8,128)(2,1)} %param.5) | copy-start | bytes 903172
  21.7 18.2 %copy-start.3 = (bf16[196,768]{1,0:T(8,128)(2,1)S(1)}, bf16[196,768]{1,0:T(8,128)(2,1)}, u32[]{:S(2)}) copy-start(bf16[196,768]{1,0:T(8,128)(2,1)} %param.6) | copy-start | bytes 903172
  21.7 18.2 %copy-start.4 = (bf16[768,32]{0,1:T(8,128)(2,1)S(1)}, bf16[768,32]{0,1:T(8,128)(2,1)}, u32[]{:S(2)}) copy-start(bf16[768,32]{0,1:T(8,128)(2,1)} %param.7) | copy-start | bytes 147460
  41.4 12.3 %all-to-all-start.2 = ((f32[32,4,192]{2,1,0:T(4,128)}), f32[32,4,192]{2,1,0:T(4,128)S(1)}, u32[]{:S(2)}, u32[]{:S(2)}) async-start(f32[32,4,192]{2,1,0:T(4,128)} %bitcast.6), calls=%async_computation.2 | async-start | bytes 262144 | tf_op jit(solution)/shard_map/all_to_all | solution.py:147

commit v4 on v3

--- a/solution.py
+++ b/solution.py
@@ -72,7 +72,7 @@
             sent[:, copy, image] = both
 
 
-def experts_kernel(dims, received, weight_in, weight_out, parts, rows_out, act_out, d_pre_out):
+def experts_kernel(dims, received, weight_in, weight_out, parts, rows_out, act_out, d_pre_out, turned_in, turned_out):
     images, local_experts, chunk = dims
     devices, per_source, width = received.shape
     shape = (chunk, images, 2, local_experts, SLOTS)
@@ -80,6 +80,9 @@
     part = size // (2 * local_experts)
     to_expert = (2, 3, 0, 1, 4)
     order = reorder(shape, to_expert, size)
+    for e in range(local_experts):
+        turned_out[e] = weight_out[e].T
+        turned_in[e] = weight_in[e].T
     moved = tuple(shape[axis] for axis in to_expert)
     back = reorder(moved, tuple(to_expert.index(axis) for axis in range(5)), size)
     for start in range(0, devices, chunk):
@@ -93,7 +96,7 @@
             rows_out[0, expert, base : base + part] = slot_in
             rows_out[1, expert, base : base + part] = slot_grad
             pre = dot(slot_in, weight_in[expert])
-            d_act = dot(slot_grad, weight_out[expert], NT)
+            d_act = dot(slot_grad, turned_out[expert])
             half = 0.5 * (1.0 + lax.erf(pre * 0.7071067811865476))
             act = (pre * half).astype(BF16)
             slope = half + pre * jnp.exp(-0.5 * pre * pre) * 0.3989422804014327
@@ -101,7 +104,7 @@
             act_out[expert, base : base + part] = act
             d_pre_out[expert, base : base + part] = d_pre
             forwards.append(dot(act, weight_out[expert]).astype(BF16))
-            backwards.append(dot(d_pre, weight_in[expert], NT).astype(BF16))
+            backwards.append(dot(d_pre, turned_in[expert]).astype(BF16))
         results = dot(back, jnp.concatenate(forwards + backwards, axis=0)).astype(BF16)
         parts[start : start + chunk] = results.reshape(chunk, per_source, width)
 
@@ -111,7 +114,7 @@
     grad_out[0] = dot(act[0], rows[1, 0], TN).astype(BF16)
 
 
-def images_kernel(dims, logits_in, tokens, out_grad, router, parts, token_grad, terms):
+def images_kernel(dims, logits_in, tokens, out_grad, parts, terms, left_out, right_out):
     n_expert, n_hidden, local_slots = dims
     images, _, width = tokens.shape
     slots = n_expert * local_slots
@@ -134,13 +137,19 @@
         d_logits = (from_combine + from_dispatch).astype(BF16)
         term = dot(d_logits, tokens[image])
         total = term if total is None else total + term
-        left = jnp.concatenate([dispatch.astype(BF16), d_logits], axis=0)
-        right = jnp.concatenate([slot_in_grad, router[...]], axis=0)
-        token_grad[image] = dot(left, right, TN).astype(BF16)
+        left_out[image, :slots] = dispatch.astype(BF16)
+        left_out[image, slots:] = d_logits
+        right_out[image] = slot_in_grad
     block = width // n_hidden
     for part in range(n_hidden):
         columns = total[:, part * block : (part + 1) * block]
-        terms[:, part] = columns.reshape(n_expert, local_slots, block)
+        terms[:, part] = columns.reshape(n_expert, local_slots, block).astype(BF16)
+
+
+def tokens_kernel(left, slot_in_grad, router, token_grad):
+    for image in range(left.shape[0]):
+        right = jnp.concatenate([slot_in_grad[image], router[...]], axis=0)
+        token_grad[image] = dot(left[image], right, TN).astype(BF16)
 
 
 def exchange(blocks):
@@ -201,6 +210,7 @@
         ),
         (received, weight_in, weight_out),
         8 * local_experts * rows * width * hidden,
+        scratch_shapes=[pltpu.VMEM((local_experts, hidden, width), BF16), pltpu.VMEM((local_experts, width, hidden), BF16)],
     )
     back = exchange(parts)
     grad_in, grad_out = call(
@@ -222,23 +232,29 @@
             pl.BlockSpec((1, hidden, width), lambda e: (e, 0, 0)),
         ],
     )
-    token_grad, terms = call(
+    terms, left, slot_in_grad = call(
         functools.partial(images_kernel, dims),
         (
-            shape((images, TOK, width), BF16),
-            shape((n_expert, n_hidden, local_slots, width // n_hidden), F32),
+            shape((n_expert, n_hidden, local_slots, width // n_hidden), BF16),
+            shape((images, 2 * slots, TOK), BF16),
+            shape((images, slots, width), BF16),
         ),
         (
             logits,
             inputs,
             out_grads,
-            router,
             back.reshape(n_expert, n_hidden, images, 2 * local_slots, width),
         ),
-        10 * images * slots * TOK * width,
+        6 * images * slots * TOK * width,
+    )
+    (token_grad,) = call(
+        tokens_kernel,
+        (shape((images, TOK, width), BF16),),
+        (left, slot_in_grad, router),
+        4 * images * slots * TOK * width,
     )
     router_parts = exchange(terms.reshape(devices, local_slots, width // n_hidden))
-    router_grad = jnp.sum(router_parts, axis=0).T
+    router_grad = jnp.sum(router_parts.astype(F32), axis=0).T
     return token_grad.reshape(images * TOK, width), router_grad, grad_in, grad_out
 
 

time: 54.5 us -> 52.5 us (0.963)
  waiting for transfers between devices: 5.53 us -> 3.63 us
    all_to_all x1, waiting for transfers between devices: 5.53 us -> 3.63 us  [exchange(): return lax.all_to_all(blocks, BOTH, split_axis=0, concat_axis=0, tiled=True)]
    pallas_call x4 -> x5, Pallas kernels: 9.11 us -> 9.05 us  [call(): pl.pallas_call(kernel, out_shape=outs, cost_estimate=pl.CostEstimate(flop...]
  transfers between devices with their start and end apart: 1 -> 1, of which waited for: 1 -> 1; matrix products, arithmetic and copies ran while one was open for 0% -> 0% of each run, Pallas kernels for 5% -> 7%
where the time goes in v4:
time: 52.5 us; the launch traced here: 52.3 us
  blocking collectives  34.4 us (66%)
  Pallas kernels  9.05 us (17%)
  starting transfers between devices  3.86 us (7%)
  waiting for transfers between devices  3.63 us (7%)
  between operations  0.69 us (1%)
  other arithmetic  0.64 us (1%)
    all_to_all x2, blocking collectives, exchange(): return lax.all_to_all(blocks, BOTH, split_axis=0, concat_axis=0, tiled=True)  34.4 us
    pallas_call x5, Pallas kernels, call(): pl.pallas_call(kernel, out_shape=outs, cost_estimate=pl.CostEstimate(flop...  9.05 us
    all_to_all x1, starting transfers between devices, exchange(): return lax.all_to_all(blocks, BOTH, split_axis=0, concat_axis=0, tiled=True)  3.86 us
    all_to_all x1, waiting for transfers between devices, exchange(): return lax.all_to_all(blocks, BOTH, split_axis=0, concat_axis=0, tiled=True)  3.63 us
  transfers between devices with their start and end apart: 1, of which 1 were waited for; matrix products, arithmetic and copies ran while one was open for 0% of the time, Pallas kernels for 7%

profile of v4, /device:TPU:0, one launch (start us, length us, event | category | flops | bytes accessed | tf_op | source)
XLA Modules:
  0.0 52.3 jit_solution(14873344287819747447)
XLA Ops:
  0.6 0.0 copy-start
  0.6 0.0 copy-start.1
  0.7 2.1 %shard_map.84 = (f32[1,32,196]{2,1,0:T(8,128)S(1)}, bf16[8,4,1,8,768]{4,3,2,1,0:T(8,128)(2,1)S(1)}) custom-call(bf16[1,196,768]{2,1,0:T(8,128)(2,1)} %bitcast.10, bf16[1,196,768]{2,1,0:T(8,128)(2,1)} %bitcast.12, bf16[32,768]{1,0:T(8,128)(2,1)} %bitcast.14), custom_call_target="tpu_custom_call" | custom-call | flops 4831838208 | bytes 1069568 | tf_op jit(solution)/shard_map/pallas_call | solution.py:161
  2.8 18.9 %all_to_all.15.received = bf16[32,8,768]{2,1,0:T(8,128)(2,1)S(1)} all-to-all(bf16[32,8,768]{2,1,0:T(8,128)(2,1)S(1)} %bitcast.9), channel_id=1, replica_groups=mesh['expert'=8,'hidden'=4] {'expert','hidden'}, dimensions={0} | all-to-all | bytes 786432 | tf_op jit(solution)/shard_map/all_to_all | solution.py:156
  21.7 0.0 copy-done
  21.7 0.0 copy-done.1
  21.7 0.0 copy-start.2
  21.7 0.0 copy-start.3
  21.7 1.7 %shard_map.85 = (bf16[32,8,768]{2,1,0:T(8,128)(2,1)S(1)}, bf16[2,2,64,768]{3,2,1,0:T(8,128)(2,1)S(1)}, bf16[2,64,768]{2,1,0:T(8,128)(2,1)S(1)}, bf16[2,64,768]{2,1,0:T(8,128)(2,1)S(1)}) custom-call(bf16[32,8,768]{2,1,0:T(8,128)(2,1)S(1)} %all_to_all.15.received, bf16[2,768,768]{2,1,0:T(8,128)(2,1)S(1)} %copy-done, bf16[2,768,768]{2,1,0:T(8,128)(2,1)S(1)} %copy-done.1), custom_call_target="tpu_custom_call" | custom-call | flops 603979776 | bytes 6291456 | tf_op jit(solution)/shard_map/pallas_call | solution.py:161
  23.5 0.0 copy-start.4
  23.5 15.5 %all_to_all.16 = bf16[32,8,768]{2,1,0:T(8,128)(2,1)S(1)} all-to-all(bf16[32,8,768]{2,1,0:T(8,128)(2,1)S(1)} %get-tuple-element.17), channel_id=1, replica_groups=mesh['expert'=8,'hidden'=4] {'expert','hidden'}, dimensions={0} | all-to-all | bytes 786432 | tf_op jit(solution)/shard_map/all_to_all | solution.py:156
  39.0 0.0 copy-done.2
  39.0 0.0 copy-done.3
  39.0 1.3 %shard_map.86 = (bf16[8,4,4,192]{3,2,1,0:T(4,128)(2,1)}, bf16[1,64,196]{2,1,0:T(8,128)(2,1)S(1)}, bf16[1,32,768]{2,1,0:T(8,128)(2,1)S(1)}) custom-call(f32[1,32,196]{2,1,0:T(8,128)S(1)} %get-tuple-element.15.logits_in, bf16[1,196,768]{2,1,0:T(8,128)(2,1)S(1)} %bitcast.11, bf16[1,196,768]{2,1,0:T(8,128)(2,1)S(1)} %bitcast.13, ...), custom_call_target="tpu_custom_call" | custom-call | flops 28901376 | bytes 1143808 | tf_op jit(solution)/shard_map/pallas_call | solution.py:161
  40.3 3.9 %all-to-all-start.2 = ((bf16[32,4,192]{2,1,0:T(4,128)(2,1)}), bf16[32,4,192]{2,1,0:T(4,128)(2,1)S(1)}, u32[]{:S(2)}, u32[]{:S(2)}) async-start(bf16[32,4,192]{2,1,0:T(4,128)(2,1)} %bitcast.6), calls=%async_computation.2 | async-start | bytes 131072 | tf_op jit(solution)/shard_map/all_to_all | solution.py:156
  44.2 2.9 %shard_map.88 = (bf16[2,768,768]{2,1,0:T(8,128)(2,1)}, bf16[2,768,768]{2,1,0:T(8,128)(2,1)}) custom-call(bf16[2,2,64,768]{3,2,1,0:T(8,128)(2,1)S(1)} %get-tuple-element.21.rows, bf16[2,64,768]{2,1,0:T(8,128)(2,1)S(1)} %get-tuple-element.22.act, bf16[2,64,768]{2,1,0:T(8,128)(2,1)S(1)} %get-tuple-element.23.d_pre), custom_call_target="tpu_custom_call" | custom-call | flops 301989888 | bytes 5505024 | tf_op jit(solution)/shard_map/pallas_call | solution.py:161
  47.0 0.0 copy-done.4
  47.1 1.0 %shard_map.87 = bf16[1,196,768]{2,1,0:T(8,128)(2,1)} custom-call(bf16[1,64,196]{2,1,0:T(8,128)(2,1)S(1)} %get-tuple-element.18.left, bf16[1,32,768]{2,1,0:T(8,128)(2,1)S(1)} %get-tuple-element.19.slot_in_grad, bf16[32,768]{1,0:T(8,128)(2,1)S(1)} %bitcast.15), custom_call_target="tpu_custom_call" | custom-call | flops 19267584 | bytes 424448 | tf_op jit(solution)/shard_map/pallas_call | solution.py:161
  48.0 3.6 %all-to-all-done.2 = bf16[32,4,192]{2,1,0:T(4,128)(2,1)S(1)} async-done(((bf16[32,4,192]{2,1,0:T(4,128)(2,1)}), bf16[32,4,192]{2,1,0:T(4,128)(2,1)S(1)}, u32[]{:S(2)}, u32[]{:S(2)}) %all-to-all-start.2) | async-done | bytes 49184 | tf_op jit(solution)/shard_map/all_to_all | solution.py:156
  51.7 0.6 %convert_reduce_fusion = f32[4,192]{1,0:T(4,128)} fusion(bf16[32,4,192]{2,1,0:T(4,128)(2,1)S(1)} %all-to-all-done.2), kind=kLoop, calls=%fused_computation | loop fusion | flops 48384 | bytes 52224 | tf_op jit(solution)/shard_map/reduce_sum | solution.py:257
Async XLA Ops:
  0.6 21.1 %copy-start = (bf16[2,768,768]{2,1,0:T(8,128)(2,1)S(1)}, bf16[2,768,768]{2,1,0:T(8,128)(2,1)}, u32[]{:S(2)}) copy-start(bf16[2,768,768]{2,1,0:T(8,128)(2,1)} %weight_in.1) | copy-start | bytes 7077892
  0.6 21.1 %copy-start.1 = (bf16[2,768,768]{2,1,0:T(8,128)(2,1)S(1)}, bf16[2,768,768]{2,1,0:T(8,128)(2,1)}, u32[]{:S(2)}) copy-start(bf16[2,768,768]{2,1,0:T(8,128)(2,1)} %weight_out.1) | copy-start | bytes 7077892
  21.7 17.3 %copy-start.2 = (bf16[196,768]{1,0:T(8,128)(2,1)S(1)}, bf16[196,768]{1,0:T(8,128)(2,1)}, u32[]{:S(2)}) copy-start(bf16[196,768]{1,0:T(8,128)(2,1)} %param.5) | copy-start | bytes 903172
  21.7 17.3 %copy-start.3 = (bf16[196,768]{1,0:T(8,128)(2,1)S(1)}, bf16[196,768]{1,0:T(8,128)(2,1)}, u32[]{:S(2)}) copy-start(bf16[196,768]{1,0:T(8,128)(2,1)} %param.6) | copy-start | bytes 903172
  23.5 23.6 %copy-start.4 = (bf16[768,32]{0,1:T(8,128)(2,1)S(1)}, bf16[768,32]{0,1:T(8,128)(2,1)}, u32[]{:S(2)}) copy-start(bf16[768,32]{0,1:T(8,128)(2,1)} %param.7) | copy-start | bytes 147460
  40.3 11.4 %all-to-all-start.2 = ((bf16[32,4,192]{2,1,0:T(4,128)(2,1)}), bf16[32,4,192]{2,1,0:T(4,128)(2,1)S(1)}, u32[]{:S(2)}, u32[]{:S(2)}) async-start(bf16[32,4,192]{2,1,0:T(4,128)(2,1)} %bitcast.6), calls=%async_computation.2 | async-start | bytes 131072 | tf_op jit(solution)/shard_map/all_to_all | solution.py:156

commit v5 on v4

--- a/solution.py
+++ b/solution.py
@@ -50,26 +50,26 @@
     copies = [
         pltpu.make_async_copy(source, target, sems.at[i])
         for i, (source, target) in enumerate(
-            ((router_hbm, router), (tokens_hbm, tokens), (out_grad_hbm, out_grad))
+            ((tokens_hbm, tokens), (router_hbm, router), (out_grad_hbm, out_grad))
         )
     ]
     for copy in copies:
         copy.start()
-    order = reorder((2, n_expert, local_slots), (1, 0, 2), 2 * slots)
     copies[0].wait()
     copies[1].wait()
     for image in range(images):
-        logits = dot(router[...], tokens[image], NT)
+        logits = dot(router[...], tokens[image].T)
         logits_out[image] = logits
         dispatch, combine = softmaxes(logits)
         slot_in = dot(dispatch.astype(BF16), tokens[image]).astype(BF16)
         if image == 0:
             copies[2].wait()
         slot_grad = dot(combine.astype(BF16), out_grad[image]).astype(BF16)
-        both = dot(order, jnp.concatenate([slot_in, slot_grad], axis=0)).astype(BF16)
-        both = both.reshape(n_expert, 2 * local_slots, width)
-        for copy in range(n_hidden):
-            sent[:, copy, image] = both
+        for expert in range(n_expert):
+            own = slice(expert * local_slots, (expert + 1) * local_slots)
+            block = jnp.concatenate([slot_in[own], slot_grad[own]], axis=0)
+            for copy in range(n_hidden):
+                sent[expert, copy, image] = block
 
 
 def experts_kernel(dims, received, weight_in, weight_out, parts, rows_out, act_out, d_pre_out, turned_in, turned_out):
@@ -118,32 +118,30 @@
     n_expert, n_hidden, local_slots = dims
     images, _, width = tokens.shape
     slots = n_expert * local_slots
-    order = reorder((n_expert, 2, local_slots), (1, 0, 2), 2 * slots)
-    total = None
+    block = width // n_hidden
+    totals = [jnp.zeros((slots, block), F32)] * n_hidden
     for image in range(images):
         dispatch, combine = softmaxes(logits_in[image])
         summed = parts[:, 0, image].astype(F32)
         for part in range(1, n_hidden):
             summed = summed + parts[:, part, image].astype(F32)
-        summed = summed.reshape(2 * slots, width).astype(BF16)
-        both = dot(order, summed).astype(BF16)
-        slot_out, slot_in_grad = both[:slots], both[slots:]
-        d_combine = dot(slot_out, out_grad[image], NT)
-        d_dispatch = dot(slot_in_grad, tokens[image], NT)
+        slot_out = summed[:, :local_slots].reshape(slots, width).astype(BF16)
+        slot_in_grad = summed[:, local_slots:].reshape(slots, width).astype(BF16)
+        d_combine = dot(slot_out, out_grad[image].T)
+        d_dispatch = dot(slot_in_grad, tokens[image].T)
         from_combine = combine * (d_combine - jnp.sum(combine * d_combine, axis=0, keepdims=True))
         from_dispatch = dispatch * (
             d_dispatch - jnp.sum(dispatch * d_dispatch, axis=1, keepdims=True)
         )
         d_logits = (from_combine + from_dispatch).astype(BF16)
-        term = dot(d_logits, tokens[image])
-        total = term if total is None else total + term
+        for part in range(n_hidden):
+            columns = tokens[image, :, part * block : (part + 1) * block]
+            totals[part] = totals[part] + dot(d_logits, columns)
         left_out[image, :slots] = dispatch.astype(BF16)
         left_out[image, slots:] = d_logits
         right_out[image] = slot_in_grad
-    block = width // n_hidden
     for part in range(n_hidden):
-        columns = total[:, part * block : (part + 1) * block]
-        terms[:, part] = columns.reshape(n_expert, local_slots, block).astype(BF16)
+        terms[:, part] = totals[part].reshape(n_expert, local_slots, block).astype(BF16)
 
 
 def tokens_kernel(left, slot_in_grad, router, token_grad):
@@ -189,7 +187,7 @@
             shape((n_expert, n_hidden, images, 2 * local_slots, width), BF16),
         ),
         tuple(pltpu.with_memory_space_constraint(x, pltpu.HBM) for x in (inputs, out_grads, router)),
-        8 * local_experts * rows * width * hidden * n_expert,
+        6 * images * slots * TOK * width,
         in_specs=[pl.BlockSpec(memory_space=pltpu.HBM)] * 3,
         scratch_shapes=[
             pltpu.VMEM(inputs.shape, BF16),
@@ -197,6 +195,15 @@
             pltpu.VMEM(router.shape, BF16),
             pltpu.SemaphoreType.DMA((3,)),
         ],
+    )
+    (sent,) = call(
+        lambda given, kept: None,
+        (shape(sent.shape, BF16),),
+        (sent,),
+        8 * local_experts * rows * width * hidden * n_expert,
+        in_specs=[pl.BlockSpec(memory_space=pl.ANY)],
+        out_specs=[pl.BlockSpec(memory_space=pl.ANY)],
+        input_output_aliases={0: 0},
     )
     received = exchange(sent.reshape(devices, per_source, width))
     chunk = max(c for c in range(1, devices + 1) if devices % c == 0 and c * per_source <= 256)

time: 52.5 us -> 52.1 us (level)
    pallas_call x5 -> x6, Pallas kernels: 9.05 us -> 8.61 us  [call(): pl.pallas_call(kernel, out_shape=outs, cost_estimate=pl.CostEstimate(flop...]
where the time goes in v5:
time: 52.1 us; the launch traced here: 51.9 us
  blocking collectives  34.4 us (66%)
  Pallas kernels  8.61 us (17%)
  starting transfers between devices  3.86 us (7%)
  waiting for transfers between devices  3.63 us (7%)
  between operations  0.7 us (1%)
  other arithmetic  0.64 us (1%)
    all_to_all x2, blocking collectives, exchange(): return lax.all_to_all(blocks, BOTH, split_axis=0, concat_axis=0, tiled=True)  34.4 us
    pallas_call x6, Pallas kernels, call(): pl.pallas_call(kernel, out_shape=outs, cost_estimate=pl.CostEstimate(flop...  8.61 us
    all_to_all x1, starting transfers between devices, exchange(): return lax.all_to_all(blocks, BOTH, split_axis=0, concat_axis=0, tiled=True)  3.86 us
    all_to_all x1, waiting for transfers between devices, exchange(): return lax.all_to_all(blocks, BOTH, split_axis=0, concat_axis=0, tiled=True)  3.63 us
  transfers between devices with their start and end apart: 1, of which 1 were waited for; matrix products, arithmetic and copies ran while one was open for 0% of the time, Pallas kernels for 7%

profile of v5, /device:TPU:0, one launch (start us, length us, event | category | flops | bytes accessed | tf_op | source)
XLA Modules:
  0.0 51.9 jit_solution(9835055486156241870)
XLA Ops:
  0.6 1.8 %shard_map.84 = (f32[1,32,196]{2,1,0:T(8,128)S(1)}, bf16[8,4,1,8,768]{4,3,2,1,0:T(8,128)(2,1)S(1)}) custom-call(bf16[1,196,768]{2,1,0:T(8,128)(2,1)} %bitcast.9, bf16[1,196,768]{2,1,0:T(8,128)(2,1)} %bitcast.11, bf16[32,768]{1,0:T(8,128)(2,1)} %bitcast.14), custom_call_target="tpu_custom_call" | custom-call | flops 28901376 | bytes 1069568 | tf_op jit(solution)/shard_map/pallas_call | solution.py:159
  2.5 0.0 copy-start
  2.5 0.0 copy-start.1
  2.5 18.9 %all_to_all.15.received = bf16[32,8,768]{2,1,0:T(8,128)(2,1)S(1)} all-to-all(bf16[32,8,768]{2,1,0:T(8,128)(2,1)S(1)} %bitcast.13), channel_id=1, replica_groups=mesh['expert'=8,'hidden'=4] {'expert','hidden'}, dimensions={0} | all-to-all | bytes 786432 | tf_op jit(solution)/shard_map/all_to_all | solution.py:154
  21.4 0.0 copy-done
  21.4 0.0 copy-done.1
  21.4 0.0 copy-start.2
  21.4 0.0 copy-start.3
  21.4 1.7 %shard_map.86 = (bf16[32,8,768]{2,1,0:T(8,128)(2,1)S(1)}, bf16[2,2,64,768]{3,2,1,0:T(8,128)(2,1)S(1)}, bf16[2,64,768]{2,1,0:T(8,128)(2,1)S(1)}, bf16[2,64,768]{2,1,0:T(8,128)(2,1)S(1)}) custom-call(bf16[32,8,768]{2,1,0:T(8,128)(2,1)S(1)} %all_to_all.15.received, bf16[2,768,768]{2,1,0:T(8,128)(2,1)S(1)} %copy-done, bf16[2,768,768]{2,1,0:T(8,128)(2,1)S(1)} %copy-done.1), custom_call_target="tpu_custom_call" | custom-call | flops 603979776 | bytes 6291456 | tf_op jit(solution)/shard_map/pallas_call | solution.py:159
  23.2 0.0 copy-start.4
  23.2 15.5 %all_to_all.16 = bf16[32,8,768]{2,1,0:T(8,128)(2,1)S(1)} all-to-all(bf16[32,8,768]{2,1,0:T(8,128)(2,1)S(1)} %get-tuple-element.17), channel_id=1, replica_groups=mesh['expert'=8,'hidden'=4] {'expert','hidden'}, dimensions={0} | all-to-all | bytes 786432 | tf_op jit(solution)/shard_map/all_to_all | solution.py:154
  38.7 0.0 copy-done.2
  38.7 0.0 copy-done.3
  38.7 1.2 %shard_map.87 = (bf16[8,4,4,192]{3,2,1,0:T(4,128)(2,1)}, bf16[1,64,196]{2,1,0:T(8,128)(2,1)S(1)}, bf16[1,32,768]{2,1,0:T(8,128)(2,1)S(1)}) custom-call(f32[1,32,196]{2,1,0:T(8,128)S(1)} %get-tuple-element.15.logits_in, bf16[1,196,768]{2,1,0:T(8,128)(2,1)S(1)} %bitcast.10, bf16[1,196,768]{2,1,0:T(8,128)(2,1)S(1)} %bitcast.12, ...), custom_call_target="tpu_custom_call" | custom-call | flops 28901376 | bytes 1143808 | tf_op jit(solution)/shard_map/pallas_call | solution.py:159
  39.9 3.9 %all-to-all-start.2 = ((bf16[32,4,192]{2,1,0:T(4,128)(2,1)}), bf16[32,4,192]{2,1,0:T(4,128)(2,1)S(1)}, u32[]{:S(2)}, u32[]{:S(2)}) async-start(bf16[32,4,192]{2,1,0:T(4,128)(2,1)} %bitcast.6), calls=%async_computation.2 | async-start | bytes 131072 | tf_op jit(solution)/shard_map/all_to_all | solution.py:154
  43.7 2.9 %shard_map.89 = (bf16[2,768,768]{2,1,0:T(8,128)(2,1)}, bf16[2,768,768]{2,1,0:T(8,128)(2,1)}) custom-call(bf16[2,2,64,768]{3,2,1,0:T(8,128)(2,1)S(1)} %get-tuple-element.21.rows, bf16[2,64,768]{2,1,0:T(8,128)(2,1)S(1)} %get-tuple-element.22.act, bf16[2,64,768]{2,1,0:T(8,128)(2,1)S(1)} %get-tuple-element.23.d_pre), custom_call_target="tpu_custom_call" | custom-call | flops 301989888 | bytes 5505024 | tf_op jit(solution)/shard_map/pallas_call | solution.py:159
  46.6 0.0 copy-done.4
  46.6 1.0 %shard_map.88 = bf16[1,196,768]{2,1,0:T(8,128)(2,1)} custom-call(bf16[1,64,196]{2,1,0:T(8,128)(2,1)S(1)} %get-tuple-element.18.left, bf16[1,32,768]{2,1,0:T(8,128)(2,1)S(1)} %get-tuple-element.19.slot_in_grad, bf16[32,768]{1,0:T(8,128)(2,1)S(1)} %bitcast.15), custom_call_target="tpu_custom_call" | custom-call | flops 19267584 | bytes 424448 | tf_op jit(solution)/shard_map/pallas_call | solution.py:159
  47.6 3.6 %all-to-all-done.2 = bf16[32,4,192]{2,1,0:T(4,128)(2,1)S(1)} async-done(((bf16[32,4,192]{2,1,0:T(4,128)(2,1)}), bf16[32,4,192]{2,1,0:T(4,128)(2,1)S(1)}, u32[]{:S(2)}, u32[]{:S(2)}) %all-to-all-start.2) | async-done | bytes 49184 | tf_op jit(solution)/shard_map/all_to_all | solution.py:154
  51.2 0.6 %convert_reduce_fusion = f32[4,192]{1,0:T(4,128)} fusion(bf16[32,4,192]{2,1,0:T(4,128)(2,1)S(1)} %all-to-all-done.2), kind=kLoop, calls=%fused_computation | loop fusion | flops 48384 | bytes 52224 | tf_op jit(solution)/shard_map/reduce_sum | solution.py:264
  (1 shorter events, 0.0 us)
Async XLA Ops:
  2.5 19.0 %copy-start = (bf16[2,768,768]{2,1,0:T(8,128)(2,1)S(1)}, bf16[2,768,768]{2,1,0:T(8,128)(2,1)}, u32[]{:S(2)}) copy-start(bf16[2,768,768]{2,1,0:T(8,128)(2,1)} %weight_in.1) | copy-start | bytes 7077892
  2.5 19.0 %copy-start.1 = (bf16[2,768,768]{2,1,0:T(8,128)(2,1)S(1)}, bf16[2,768,768]{2,1,0:T(8,128)(2,1)}, u32[]{:S(2)}) copy-start(bf16[2,768,768]{2,1,0:T(8,128)(2,1)} %weight_out.1) | copy-start | bytes 7077892
  21.4 17.3 %copy-start.2 = (bf16[196,768]{1,0:T(8,128)(2,1)S(1)}, bf16[196,768]{1,0:T(8,128)(2,1)}, u32[]{:S(2)}) copy-start(bf16[196,768]{1,0:T(8,128)(2,1)} %param.5) | copy-start | bytes 903172
  21.4 17.3 %copy-start.3 = (bf16[196,768]{1,0:T(8,128)(2,1)S(1)}, bf16[196,768]{1,0:T(8,128)(2,1)}, u32[]{:S(2)}) copy-start(bf16[196,768]{1,0:T(8,128)(2,1)} %param.6) | copy-start | bytes 903172
  23.2 23.4 %copy-start.4 = (bf16[768,32]{0,1:T(8,128)(2,1)S(1)}, bf16[768,32]{0,1:T(8,128)(2,1)}, u32[]{:S(2)}) copy-start(bf16[768,32]{0,1:T(8,128)(2,1)} %param.7) | copy-start | bytes 147460
  39.9 11.4 %all-to-all-start.2 = ((bf16[32,4,192]{2,1,0:T(4,128)(2,1)}), bf16[32,4,192]{2,1,0:T(4,128)(2,1)S(1)}, u32[]{:S(2)}, u32[]{:S(2)}) async-start(bf16[32,4,192]{2,1,0:T(4,128)(2,1)} %bitcast.6), calls=%async_computation.2 | async-start | bytes 131072 | tf_op jit(solution)/shard_map/all_to_all | solution.py:154

commit v6 on v5

--- a/solution.py
+++ b/solution.py
@@ -1,4 +1,5 @@
 import functools
+import math
 
 import jax
 import jax.numpy as jnp
@@ -10,6 +11,7 @@
 SLOTS = 2
 TOK = 196
 BOTH = ("expert", "hidden")
+STRIDES = (19, 3, 15)
 F32, BF16 = jnp.float32, jnp.bfloat16
 NN = (((1,), (0,)), ((), ()))
 NT = (((1,), (1,)), ((), ()))
@@ -34,6 +36,16 @@
     return jnp.where(columns == source, 1.0, 0.0).astype(BF16)
 
 
+def ring(devices, stride):
+    if math.gcd(devices, stride) != 1:
+        stride = 1
+    return [stride * place % devices for place in range(devices)]
+
+
+def places(devices, stride):
+    return {device: place for place, device in enumerate(ring(devices, stride))}
+
+
 def softmaxes(logits):
     by_token = jnp.exp(logits - jnp.max(logits, axis=1, keepdims=True))
     dispatch = by_token / jnp.sum(by_token, axis=1, keepdims=True)
@@ -46,7 +58,7 @@
     tokens, out_grad, router, sems = scratch
     n_expert, n_hidden, local_slots = dims
     images, _, width = tokens.shape
-    slots = n_expert * local_slots
+    place = places(n_expert * n_hidden, STRIDES[0])
     copies = [
         pltpu.make_async_copy(source, target, sems.at[i])
         for i, (source, target) in enumerate(
@@ -68,13 +80,14 @@
         for expert in range(n_expert):
             own = slice(expert * local_slots, (expert + 1) * local_slots)
             block = jnp.concatenate([slot_in[own], slot_grad[own]], axis=0)
-            for copy in range(n_hidden):
-                sent[expert, copy, image] = block
+            for part in range(n_hidden):
+                sent[place[expert * n_hidden + part], image] = block
 
 
 def experts_kernel(dims, received, weight_in, weight_out, parts, rows_out, act_out, d_pre_out, turned_in, turned_out):
     images, local_experts, chunk = dims
     devices, per_source, width = received.shape
+    source, place = ring(devices, STRIDES[0]), places(devices, STRIDES[1])
     shape = (chunk, images, 2, local_experts, SLOTS)
     size = chunk * per_source
     part = size // (2 * local_experts)
@@ -106,7 +119,9 @@
             forwards.append(dot(act, weight_out[expert]).astype(BF16))
             backwards.append(dot(d_pre, turned_in[expert]).astype(BF16))
         results = dot(back, jnp.concatenate(forwards + backwards, axis=0)).astype(BF16)
-        parts[start : start + chunk] = results.reshape(chunk, per_source, width)
+        results = results.reshape(chunk, per_source, width)
+        for row in range(chunk):
+            parts[place[source[start + row]]] = results[row]
 
 
 def weights_kernel(rows, act, d_pre, grad_in, grad_out):
@@ -118,13 +133,16 @@
     n_expert, n_hidden, local_slots = dims
     images, _, width = tokens.shape
     slots = n_expert * local_slots
+    place = places(n_expert * n_hidden, STRIDES[1])
     block = width // n_hidden
     totals = [jnp.zeros((slots, block), F32)] * n_hidden
     for image in range(images):
         dispatch, combine = softmaxes(logits_in[image])
-        summed = parts[:, 0, image].astype(F32)
-        for part in range(1, n_hidden):
-            summed = summed + parts[:, part, image].astype(F32)
+        summed = []
+        for expert in range(n_expert):
+            held = [parts[place[expert * n_hidden + part], image] for part in range(n_hidden)]
+            summed.append(sum(piece.astype(F32) for piece in held))
+        summed = jnp.stack(summed)
         slot_out = summed[:, :local_slots].reshape(slots, width).astype(BF16)
         slot_in_grad = summed[:, local_slots:].reshape(slots, width).astype(BF16)
         d_combine = dot(slot_out, out_grad[image].T)
@@ -140,8 +158,11 @@
         left_out[image, :slots] = dispatch.astype(BF16)
         left_out[image, slots:] = d_logits
         right_out[image] = slot_in_grad
+    place = places(n_expert * n_hidden, STRIDES[2])
     for part in range(n_hidden):
-        terms[:, part] = totals[part].reshape(n_expert, local_slots, block).astype(BF16)
+        for expert in range(n_expert):
+            own = slice(expert * local_slots, (expert + 1) * local_slots)
+            terms[place[expert * n_hidden + part]] = totals[part][own].astype(BF16)
 
 
 def tokens_kernel(left, slot_in_grad, router, token_grad):
@@ -150,8 +171,11 @@
         token_grad[image] = dot(left[image], right, TN).astype(BF16)
 
 
-def exchange(blocks):
-    return lax.all_to_all(blocks, BOTH, split_axis=0, concat_axis=0, tiled=True)
+def exchange(blocks, stride):
+    order = [ring(blocks.shape[0], stride)]
+    return lax.all_to_all(
+        blocks, BOTH, split_axis=0, concat_axis=0, tiled=True, axis_index_groups=order
+    )
 
 
 def call(kernel, outs, args, flops, **more):
@@ -184,7 +208,7 @@
         functools.partial(slots_kernel, dims),
         (
             shape((images, slots, TOK), F32),
-            shape((n_expert, n_hidden, images, 2 * local_slots, width), BF16),
+            shape((devices, images, 2 * local_slots, width), BF16),
         ),
         tuple(pltpu.with_memory_space_constraint(x, pltpu.HBM) for x in (inputs, out_grads, router)),
         6 * images * slots * TOK * width,
@@ -205,7 +229,7 @@
         out_specs=[pl.BlockSpec(memory_space=pl.ANY)],
         input_output_aliases={0: 0},
     )
-    received = exchange(sent.reshape(devices, per_source, width))
+    received = exchange(sent.reshape(devices, per_source, width), STRIDES[0])
     chunk = max(c for c in range(1, devices + 1) if devices % c == 0 and c * per_source <= 256)
     parts, slot_rows, act, d_pre = call(
         functools.partial(experts_kernel, (images, local_experts, chunk)),
@@ -219,7 +243,7 @@
         8 * local_experts * rows * width * hidden,
         scratch_shapes=[pltpu.VMEM((local_experts, hidden, width), BF16), pltpu.VMEM((local_experts, width, hidden), BF16)],
     )
-    back = exchange(parts)
+    back = exchange(parts, STRIDES[1])
     grad_in, grad_out = call(
         weights_kernel,
         (
@@ -242,7 +266,7 @@
     terms, left, slot_in_grad = call(
         functools.partial(images_kernel, dims),
         (
-            shape((n_expert, n_hidden, local_slots, width // n_hidden), BF16),
+            shape((devices, local_slots, width // n_hidden), BF16),
             shape((images, 2 * slots, TOK), BF16),
             shape((images, slots, width), BF16),
         ),
@@ -250,7 +274,7 @@
             logits,
             inputs,
             out_grads,
-            back.reshape(n_expert, n_hidden, images, 2 * local_slots, width),
+            back.reshape(devices, images, 2 * local_slots, width),
         ),
         6 * images * slots * TOK * width,
     )
@@ -260,7 +284,7 @@
         (left, slot_in_grad, router),
         4 * images * slots * TOK * width,
     )
-    router_parts = exchange(terms.reshape(devices, local_slots, width // n_hidden))
+    router_parts = exchange(terms, STRIDES[2])
     router_grad = jnp.sum(router_parts.astype(F32), axis=0).T
     return token_grad.reshape(images * TOK, width), router_grad, grad_in, grad_out
 

time: 52.1 us -> 51.3 us (0.985)
  starting transfers between devices: 3.86 us -> 2.57 us
  blocking collectives: 34.4 us -> 35.2 us
    all_to_all x1, starting transfers between devices: 3.86 us -> 2.57 us  [exchange(): lax.all_to_all(blocks, BOTH, split_axis=0, concat_axis=0, tiled=True, axi...]
    all_to_all x2, blocking collectives: 34.4 us -> 35.2 us  [exchange(): lax.all_to_all(blocks, BOTH, split_axis=0, concat_axis=0, tiled=True, axi...]
  transfers between devices with their start and end apart: 1 -> 1, of which waited for: 1 -> 1; matrix products, arithmetic and copies ran while one was open for 0% -> 0% of each run, Pallas kernels for 7% -> 8%
where the time goes in v6:
time: 51.3 us; the launch traced here: 51.1 us
  blocking collectives  35.2 us (69%)
  Pallas kernels  8.61 us (17%)
  waiting for transfers between devices  3.28 us (6%)
  starting transfers between devices  2.57 us (5%)
  between operations  0.7 us (1%)
  other arithmetic  0.64 us (1%)
    all_to_all x2, blocking collectives, exchange(): lax.all_to_all(blocks, BOTH, split_axis=0, concat_axis=0, tiled=True, axi...  35.2 us
    pallas_call x6, Pallas kernels, call(): pl.pallas_call(kernel, out_shape=outs, cost_estimate=pl.CostEstimate(flop...  8.61 us
    all_to_all x1, waiting for transfers between devices, exchange(): lax.all_to_all(blocks, BOTH, split_axis=0, concat_axis=0, tiled=True, axi...  3.28 us
    all_to_all x1, starting transfers between devices, exchange(): lax.all_to_all(blocks, BOTH, split_axis=0, concat_axis=0, tiled=True, axi...  2.57 us
  transfers between devices with their start and end apart: 1, of which 1 were waited for; matrix products, arithmetic and copies ran while one was open for 0% of the time, Pallas kernels for 8%

profile of v6, /device:TPU:0, one launch (start us, length us, event | category | flops | bytes accessed | tf_op | source)
XLA Modules:
  0.0 51.1 jit_solution(332827921659873136)
XLA Ops:
  0.6 1.8 %shard_map.84 = (f32[1,32,196]{2,1,0:T(8,128)S(1)}, bf16[32,1,8,768]{3,2,1,0:T(8,128)(2,1)S(1)}) custom-call(bf16[1,196,768]{2,1,0:T(8,128)(2,1)} %bitcast.8, bf16[1,196,768]{2,1,0:T(8,128)(2,1)} %bitcast.10, bf16[32,768]{1,0:T(8,128)(2,1)} %bitcast.13), custom_call_target="tpu_custom_call" | custom-call | flops 28901376 | bytes 1069568 | tf_op jit(solution)/shard_map/pallas_call | solution.py:183
  2.5 0.0 copy-start
  2.5 0.0 copy-start.1
  2.5 20.1 %all_to_all.15.received = bf16[32,8,768]{2,1,0:T(8,128)(2,1)S(1)} all-to-all(bf16[32,8,768]{2,1,0:T(8,128)(2,1)S(1)} %bitcast.12), channel_id=1, replica_groups={{0,19,6,25,12,31,18,5,24,11,30,17,4,23,10,29,16,3,22,9,28,15,2,21,8,27,..., dimensions={0} | all-to-all | bytes 786432 | tf_op jit(solution)/shard_map/all_to_all | solution.py:176
  22.6 0.0 copy-done
  22.6 0.0 copy-done.1
  22.6 0.0 copy-start.2
  22.6 0.0 copy-start.3
  22.6 1.7 %shard_map.86 = (bf16[32,8,768]{2,1,0:T(8,128)(2,1)S(1)}, bf16[2,2,64,768]{3,2,1,0:T(8,128)(2,1)S(1)}, bf16[2,64,768]{2,1,0:T(8,128)(2,1)S(1)}, bf16[2,64,768]{2,1,0:T(8,128)(2,1)S(1)}) custom-call(bf16[32,8,768]{2,1,0:T(8,128)(2,1)S(1)} %all_to_all.15.received, bf16[2,768,768]{2,1,0:T(8,128)(2,1)S(1)} %copy-done, bf16[2,768,768]{2,1,0:T(8,128)(2,1)S(1)} %copy-done.1), custom_call_target="tpu_custom_call" | custom-call | flops 603979776 | bytes 6291456 | tf_op jit(solution)/shard_map/pallas_call | solution.py:183
  24.3 0.0 copy-start.4
  24.4 15.1 %all_to_all.16 = bf16[32,8,768]{2,1,0:T(8,128)(2,1)S(1)} all-to-all(bf16[32,8,768]{2,1,0:T(8,128)(2,1)S(1)} %get-tuple-element.17), channel_id=1, replica_groups={{0,3,6,9,12,15,18,21,24,27,30,1,4,7,10,13,16,19,22,25,28,31,2,5,8,11,14..., dimensions={0} | all-to-all | bytes 786432 | tf_op jit(solution)/shard_map/all_to_all | solution.py:176
  39.5 0.0 copy-done.2
  39.5 0.0 copy-done.3
  39.5 1.2 %shard_map.87 = (bf16[32,4,192]{2,1,0:T(4,128)(2,1)}, bf16[1,64,196]{2,1,0:T(8,128)(2,1)S(1)}, bf16[1,32,768]{2,1,0:T(8,128)(2,1)S(1)}) custom-call(f32[1,32,196]{2,1,0:T(8,128)S(1)} %get-tuple-element.15.logits_in, bf16[1,196,768]{2,1,0:T(8,128)(2,1)S(1)} %bitcast.9, bf16[1,196,768]{2,1,0:T(8,128)(2,1)S(1)} %bitcast.11, bf16[32,1,8,768]{3,2,1,0:T(8,128)(2,1)S(1)} %bitcast.7), custom_call_target="tpu_custom_call" | custom-call | flops 28901376 | bytes 1143808 | tf_op jit(solution)/shard_map/pallas_call | solution.py:183
  40.7 2.6 %all-to-all-start.2 = ((bf16[32,4,192]{2,1,0:T(4,128)(2,1)}), bf16[32,4,192]{2,1,0:T(4,128)(2,1)S(1)}, u32[]{:S(2)}, u32[]{:S(2)}) async-start(bf16[32,4,192]{2,1,0:T(4,128)(2,1)} %get-tuple-element.20), calls=%async_computation.2 | async-start | bytes 131072 | tf_op jit(solution)/shard_map/all_to_all | solution.py:176
  43.3 2.9 %shard_map.89 = (bf16[2,768,768]{2,1,0:T(8,128)(2,1)}, bf16[2,768,768]{2,1,0:T(8,128)(2,1)}) custom-call(bf16[2,2,64,768]{3,2,1,0:T(8,128)(2,1)S(1)} %get-tuple-element.21.rows, bf16[2,64,768]{2,1,0:T(8,128)(2,1)S(1)} %get-tuple-element.22.act, bf16[2,64,768]{2,1,0:T(8,128)(2,1)S(1)} %get-tuple-element.23.d_pre), custom_call_target="tpu_custom_call" | custom-call | flops 301989888 | bytes 5505024 | tf_op jit(solution)/shard_map/pallas_call | solution.py:183
  46.1 0.0 copy-done.4
  46.1 1.0 %shard_map.88 = bf16[1,196,768]{2,1,0:T(8,128)(2,1)} custom-call(bf16[1,64,196]{2,1,0:T(8,128)(2,1)S(1)} %get-tuple-element.18.left, bf16[1,32,768]{2,1,0:T(8,128)(2,1)S(1)} %get-tuple-element.19.slot_in_grad, bf16[32,768]{1,0:T(8,128)(2,1)S(1)} %bitcast.14), custom_call_target="tpu_custom_call" | custom-call | flops 19267584 | bytes 424448 | tf_op jit(solution)/shard_map/pallas_call | solution.py:183
  47.1 3.3 %all-to-all-done.2 = bf16[32,4,192]{2,1,0:T(4,128)(2,1)S(1)} async-done(((bf16[32,4,192]{2,1,0:T(4,128)(2,1)}), bf16[32,4,192]{2,1,0:T(4,128)(2,1)S(1)}, u32[]{:S(2)}, u32[]{:S(2)}) %all-to-all-start.2) | async-done | bytes 49184 | tf_op jit(solution)/shard_map/all_to_all | solution.py:176
  50.4 0.6 %convert_reduce_fusion = f32[4,192]{1,0:T(4,128)} fusion(bf16[32,4,192]{2,1,0:T(4,128)(2,1)S(1)} %all-to-all-done.2), kind=kLoop, calls=%fused_computation | loop fusion | flops 48384 | bytes 52224 | tf_op jit(solution)/shard_map/reduce_sum | solution.py:288
  (1 shorter events, 0.0 us)
Async XLA Ops:
  2.5 20.1 %copy-start = (bf16[2,768,768]{2,1,0:T(8,128)(2,1)S(1)}, bf16[2,768,768]{2,1,0:T(8,128)(2,1)}, u32[]{:S(2)}) copy-start(bf16[2,768,768]{2,1,0:T(8,128)(2,1)} %weight_in.1) | copy-start | bytes 7077892
  2.5 20.1 %copy-start.1 = (bf16[2,768,768]{2,1,0:T(8,128)(2,1)S(1)}, bf16[2,768,768]{2,1,0:T(8,128)(2,1)}, u32[]{:S(2)}) copy-start(bf16[2,768,768]{2,1,0:T(8,128)(2,1)} %weight_out.1) | copy-start | bytes 7077892
  22.6 16.9 %copy-start.2 = (bf16[196,768]{1,0:T(8,128)(2,1)S(1)}, bf16[196,768]{1,0:T(8,128)(2,1)}, u32[]{:S(2)}) copy-start(bf16[196,768]{1,0:T(8,128)(2,1)} %param.5) | copy-start | bytes 903172
  22.6 16.9 %copy-start.3 = (bf16[196,768]{1,0:T(8,128)(2,1)S(1)}, bf16[196,768]{1,0:T(8,128)(2,1)}, u32[]{:S(2)}) copy-start(bf16[196,768]{1,0:T(8,128)(2,1)} %param.6) | copy-start | bytes 903172
  24.3 21.8 %copy-start.4 = (bf16[768,32]{0,1:T(8,128)(2,1)S(1)}, bf16[768,32]{0,1:T(8,128)(2,1)}, u32[]{:S(2)}) copy-start(bf16[768,32]{0,1:T(8,128)(2,1)} %param.7) | copy-start | bytes 147460
  40.7 9.7 %all-to-all-start.2 = ((bf16[32,4,192]{2,1,0:T(4,128)(2,1)}), bf16[32,4,192]{2,1,0:T(4,128)(2,1)S(1)}, u32[]{:S(2)}, u32[]{:S(2)}) async-start(bf16[32,4,192]{2,1,0:T(4,128)(2,1)} %get-tuple-element.20), calls=%async_computation.2 | async-start | bytes 131072 | tf_op jit(solution)/shard_map/all_to_all | solution.py:176

commit v7 on v6

--- a/solution.py
+++ b/solution.py
@@ -11,7 +11,6 @@
 SLOTS = 2
 TOK = 196
 BOTH = ("expert", "hidden")
-STRIDES = (19, 3, 15)
 F32, BF16 = jnp.float32, jnp.bfloat16
 NN = (((1,), (0,)), ((), ()))
 NT = (((1,), (1,)), ((), ()))
@@ -36,14 +35,27 @@
     return jnp.where(columns == source, 1.0, 0.0).astype(BF16)
 
 
-def ring(devices, stride):
+def strided(devices, stride):
     if math.gcd(devices, stride) != 1:
         stride = 1
-    return [stride * place % devices for place in range(devices)]
-
-
-def places(devices, stride):
-    return {device: place for place, device in enumerate(ring(devices, stride))}
+    return [stride * turn % devices for turn in range(devices)]
+
+
+def halves(n_expert, n_hidden):
+    return [
+        (first + n_expert // 2 * step) % n_expert * n_hidden + (-step) % n_hidden
+        for first in range(n_expert)
+        for step in range(n_hidden)
+    ]
+
+
+def orders(n_expert, n_hidden):
+    devices = n_expert * n_hidden
+    return strided(devices, 19), halves(n_expert, n_hidden), strided(devices, 15)
+
+
+def places(order):
+    return {device: place for place, device in enumerate(order)}
 
 
 def softmaxes(logits):
@@ -58,7 +70,7 @@
     tokens, out_grad, router, sems = scratch
     n_expert, n_hidden, local_slots = dims
     images, _, width = tokens.shape
-    place = places(n_expert * n_hidden, STRIDES[0])
+    place = places(orders(n_expert, n_hidden)[0])
     copies = [
         pltpu.make_async_copy(source, target, sems.at[i])
         for i, (source, target) in enumerate(
@@ -85,9 +97,9 @@
 
 
 def experts_kernel(dims, received, weight_in, weight_out, parts, rows_out, act_out, d_pre_out, turned_in, turned_out):
-    images, local_experts, chunk = dims
+    images, local_experts, chunk, order_in, order_out = dims
     devices, per_source, width = received.shape
-    source, place = ring(devices, STRIDES[0]), places(devices, STRIDES[1])
+    source, place = order_in, places(order_out)
     shape = (chunk, images, 2, local_experts, SLOTS)
     size = chunk * per_source
     part = size // (2 * local_experts)
@@ -133,7 +145,7 @@
     n_expert, n_hidden, local_slots = dims
     images, _, width = tokens.shape
     slots = n_expert * local_slots
-    place = places(n_expert * n_hidden, STRIDES[1])
+    place = places(orders(n_expert, n_hidden)[1])
     block = width // n_hidden
     totals = [jnp.zeros((slots, block), F32)] * n_hidden
     for image in range(images):
@@ -158,7 +170,7 @@
         left_out[image, :slots] = dispatch.astype(BF16)
         left_out[image, slots:] = d_logits
         right_out[image] = slot_in_grad
-    place = places(n_expert * n_hidden, STRIDES[2])
+    place = places(orders(n_expert, n_hidden)[2])
     for part in range(n_hidden):
         for expert in range(n_expert):
             own = slice(expert * local_slots, (expert + 1) * local_slots)
@@ -171,10 +183,9 @@
         token_grad[image] = dot(left[image], right, TN).astype(BF16)
 
 
-def exchange(blocks, stride):
-    order = [ring(blocks.shape[0], stride)]
+def exchange(blocks, order):
     return lax.all_to_all(
-        blocks, BOTH, split_axis=0, concat_axis=0, tiled=True, axis_index_groups=order
+        blocks, BOTH, split_axis=0, concat_axis=0, tiled=True, axis_index_groups=[order]
     )
 
 
@@ -203,6 +214,7 @@
     out_grads = out_grad.reshape(images, TOK, width)
     router = slot_router.T
     dims = (n_expert, n_hidden, local_slots)
+    order = orders(n_expert, n_hidden)
 
     logits, sent = call(
         functools.partial(slots_kernel, dims),
@@ -229,10 +241,10 @@
         out_specs=[pl.BlockSpec(memory_space=pl.ANY)],
         input_output_aliases={0: 0},
     )
-    received = exchange(sent.reshape(devices, per_source, width), STRIDES[0])
+    received = exchange(sent.reshape(devices, per_source, width), order[0])
     chunk = max(c for c in range(1, devices + 1) if devices % c == 0 and c * per_source <= 256)
     parts, slot_rows, act, d_pre = call(
-        functools.partial(experts_kernel, (images, local_experts, chunk)),
+        functools.partial(experts_kernel, (images, local_experts, chunk, *order[:2])),
         (
             shape((devices, per_source, width), BF16),
             shape((2, local_experts, rows, width), BF16),
@@ -243,7 +255,7 @@
         8 * local_experts * rows * width * hidden,
         scratch_shapes=[pltpu.VMEM((local_experts, hidden, width), BF16), pltpu.VMEM((local_experts, width, hidden), BF16)],
     )
-    back = exchange(parts, STRIDES[1])
+    back = exchange(parts, order[1])
     grad_in, grad_out = call(
         weights_kernel,
         (
@@ -284,7 +296,7 @@
         (left, slot_in_grad, router),
         4 * images * slots * TOK * width,
     )
-    router_parts = exchange(terms, STRIDES[2])
+    router_parts = exchange(terms, order[2])
     router_grad = jnp.sum(router_parts.astype(F32), axis=0).T
     return token_grad.reshape(images * TOK, width), router_grad, grad_in, grad_out
 

time: 51.3 us -> 51 us (level)
  blocking collectives: 35.2 us -> 33.9 us
  starting transfers between devices: 2.57 us -> 3.59 us
    all_to_all x2, blocking collectives: 35.2 us -> 33.9 us  [exchange(): lax.all_to_all(blocks, BOTH, split_axis=0, concat_axis=0, tiled=True, axi...]
    all_to_all x1, starting transfers between devices: 2.57 us -> 3.59 us  [exchange(): lax.all_to_all(blocks, BOTH, split_axis=0, concat_axis=0, tiled=True, axi...]
where the time goes in v7:
time: 51 us; the launch traced here: 50.7 us
  blocking collectives  33.9 us (66%)
  Pallas kernels  8.61 us (17%)
  starting transfers between devices  3.59 us (7%)
  waiting for transfers between devices  3.28 us (6%)
  between operations  0.7 us (1%)
  other arithmetic  0.64 us (1%)
    all_to_all x2, blocking collectives, exchange(): lax.all_to_all(blocks, BOTH, split_axis=0, concat_axis=0, tiled=True, axi...  33.9 us
    pallas_call x6, Pallas kernels, call(): pl.pallas_call(kernel, out_shape=outs, cost_estimate=pl.CostEstimate(flop...  8.61 us
    all_to_all x1, starting transfers between devices, exchange(): lax.all_to_all(blocks, BOTH, split_axis=0, concat_axis=0, tiled=True, axi...  3.59 us
    all_to_all x1, waiting for transfers between devices, exchange(): lax.all_to_all(blocks, BOTH, split_axis=0, concat_axis=0, tiled=True, axi...  3.28 us
  transfers between devices with their start and end apart: 1, of which 1 were waited for; matrix products, arithmetic and copies ran while one was open for 0% of the time, Pallas kernels for 8%

profile of v7, /device:TPU:0, one launch (start us, length us, event | category | flops | bytes accessed | tf_op | source)
XLA Modules:
  0.0 50.7 jit_solution(16391698955320578367)
XLA Ops:
  0.6 1.8 %shard_map.84 = (f32[1,32,196]{2,1,0:T(8,128)S(1)}, bf16[32,1,8,768]{3,2,1,0:T(8,128)(2,1)S(1)}) custom-call(bf16[1,196,768]{2,1,0:T(8,128)(2,1)} %bitcast.8, bf16[1,196,768]{2,1,0:T(8,128)(2,1)} %bitcast.10, bf16[32,768]{1,0:T(8,128)(2,1)} %bitcast.13), custom_call_target="tpu_custom_call" | custom-call | flops 28901376 | bytes 1069568 | tf_op jit(solution)/shard_map/pallas_call | solution.py:194
  2.5 0.0 copy-start
  2.5 0.0 copy-start.1
  2.5 20.1 %all_to_all.15.received = bf16[32,8,768]{2,1,0:T(8,128)(2,1)S(1)} all-to-all(bf16[32,8,768]{2,1,0:T(8,128)(2,1)S(1)} %bitcast.12), channel_id=1, replica_groups={{0,19,6,25,12,31,18,5,24,11,30,17,4,23,10,29,16,3,22,9,28,15,2,21,8,27,..., dimensions={0} | all-to-all | bytes 786432 | tf_op jit(solution)/shard_map/all_to_all | solution.py:187
  22.6 0.0 copy-done
  22.6 0.0 copy-done.1
  22.6 0.0 copy-start.2
  22.6 0.0 copy-start.3
  22.6 1.7 %shard_map.86 = (bf16[32,8,768]{2,1,0:T(8,128)(2,1)S(1)}, bf16[2,2,64,768]{3,2,1,0:T(8,128)(2,1)S(1)}, bf16[2,64,768]{2,1,0:T(8,128)(2,1)S(1)}, bf16[2,64,768]{2,1,0:T(8,128)(2,1)S(1)}) custom-call(bf16[32,8,768]{2,1,0:T(8,128)(2,1)S(1)} %all_to_all.15.received, bf16[2,768,768]{2,1,0:T(8,128)(2,1)S(1)} %copy-done, bf16[2,768,768]{2,1,0:T(8,128)(2,1)S(1)} %copy-done.1), custom_call_target="tpu_custom_call" | custom-call | flops 603979776 | bytes 6291456 | tf_op jit(solution)/shard_map/pallas_call | solution.py:194
  24.3 0.0 copy-start.4
  24.4 13.8 %all_to_all.16 = bf16[32,8,768]{2,1,0:T(8,128)(2,1)S(1)} all-to-all(bf16[32,8,768]{2,1,0:T(8,128)(2,1)S(1)} %get-tuple-element.17), channel_id=1, replica_groups={{0,19,2,17,4,23,6,21,8,27,10,25,12,31,14,29,16,3,18,1,20,7,22,5,24,11,2..., dimensions={0} | all-to-all | bytes 786432 | tf_op jit(solution)/shard_map/all_to_all | solution.py:187
  38.2 0.0 copy-done.2
  38.2 0.0 copy-done.3
  38.2 1.2 %shard_map.87 = (bf16[32,4,192]{2,1,0:T(4,128)(2,1)}, bf16[1,64,196]{2,1,0:T(8,128)(2,1)S(1)}, bf16[1,32,768]{2,1,0:T(8,128)(2,1)S(1)}) custom-call(f32[1,32,196]{2,1,0:T(8,128)S(1)} %get-tuple-element.15.logits_in, bf16[1,196,768]{2,1,0:T(8,128)(2,1)S(1)} %bitcast.9, bf16[1,196,768]{2,1,0:T(8,128)(2,1)S(1)} %bitcast.11, bf16[32,1,8,768]{3,2,1,0:T(8,128)(2,1)S(1)} %bitcast.7), custom_call_target="tpu_custom_call" | custom-call | flops 28901376 | bytes 1143808 | tf_op jit(solution)/shard_map/pallas_call | solution.py:194
  39.3 3.6 %all-to-all-start.2 = ((bf16[32,4,192]{2,1,0:T(4,128)(2,1)}), bf16[32,4,192]{2,1,0:T(4,128)(2,1)S(1)}, u32[]{:S(2)}, u32[]{:S(2)}) async-start(bf16[32,4,192]{2,1,0:T(4,128)(2,1)} %get-tuple-element.20), calls=%async_computation.2 | async-start | bytes 131072 | tf_op jit(solution)/shard_map/all_to_all | solution.py:187
  42.9 2.9 %shard_map.89 = (bf16[2,768,768]{2,1,0:T(8,128)(2,1)}, bf16[2,768,768]{2,1,0:T(8,128)(2,1)}) custom-call(bf16[2,2,64,768]{3,2,1,0:T(8,128)(2,1)S(1)} %get-tuple-element.21.rows, bf16[2,64,768]{2,1,0:T(8,128)(2,1)S(1)} %get-tuple-element.22.act, bf16[2,64,768]{2,1,0:T(8,128)(2,1)S(1)} %get-tuple-element.23.d_pre), custom_call_target="tpu_custom_call" | custom-call | flops 301989888 | bytes 5505024 | tf_op jit(solution)/shard_map/pallas_call | solution.py:194
  45.8 0.0 copy-done.4
  45.8 1.0 %shard_map.88 = bf16[1,196,768]{2,1,0:T(8,128)(2,1)} custom-call(bf16[1,64,196]{2,1,0:T(8,128)(2,1)S(1)} %get-tuple-element.18.left, bf16[1,32,768]{2,1,0:T(8,128)(2,1)S(1)} %get-tuple-element.19.slot_in_grad, bf16[32,768]{1,0:T(8,128)(2,1)S(1)} %bitcast.14), custom_call_target="tpu_custom_call" | custom-call | flops 19267584 | bytes 424448 | tf_op jit(solution)/shard_map/pallas_call | solution.py:194
  46.8 3.3 %all-to-all-done.2 = bf16[32,4,192]{2,1,0:T(4,128)(2,1)S(1)} async-done(((bf16[32,4,192]{2,1,0:T(4,128)(2,1)}), bf16[32,4,192]{2,1,0:T(4,128)(2,1)S(1)}, u32[]{:S(2)}, u32[]{:S(2)}) %all-to-all-start.2) | async-done | bytes 49184 | tf_op jit(solution)/shard_map/all_to_all | solution.py:187
  50.1 0.6 %convert_reduce_fusion = f32[4,192]{1,0:T(4,128)} fusion(bf16[32,4,192]{2,1,0:T(4,128)(2,1)S(1)} %all-to-all-done.2), kind=kLoop, calls=%fused_computation | loop fusion | flops 48384 | bytes 52224 | tf_op jit(solution)/shard_map/reduce_sum | solution.py:300
  (1 shorter events, 0.0 us)
Async XLA Ops:
  2.5 20.1 %copy-start = (bf16[2,768,768]{2,1,0:T(8,128)(2,1)S(1)}, bf16[2,768,768]{2,1,0:T(8,128)(2,1)}, u32[]{:S(2)}) copy-start(bf16[2,768,768]{2,1,0:T(8,128)(2,1)} %weight_in.1) | copy-start | bytes 7077892
  2.5 20.1 %copy-start.1 = (bf16[2,768,768]{2,1,0:T(8,128)(2,1)S(1)}, bf16[2,768,768]{2,1,0:T(8,128)(2,1)}, u32[]{:S(2)}) copy-start(bf16[2,768,768]{2,1,0:T(8,128)(2,1)} %weight_out.1) | copy-start | bytes 7077892
  22.6 15.6 %copy-start.2 = (bf16[196,768]{1,0:T(8,128)(2,1)S(1)}, bf16[196,768]{1,0:T(8,128)(2,1)}, u32[]{:S(2)}) copy-start(bf16[196,768]{1,0:T(8,128)(2,1)} %param.5) | copy-start | bytes 903172
  22.6 15.6 %copy-start.3 = (bf16[196,768]{1,0:T(8,128)(2,1)S(1)}, bf16[196,768]{1,0:T(8,128)(2,1)}, u32[]{:S(2)}) copy-start(bf16[196,768]{1,0:T(8,128)(2,1)} %param.6) | copy-start | bytes 903172
  24.3 21.5 %copy-start.4 = (bf16[768,32]{0,1:T(8,128)(2,1)S(1)}, bf16[768,32]{0,1:T(8,128)(2,1)}, u32[]{:S(2)}) copy-start(bf16[768,32]{0,1:T(8,128)(2,1)} %param.7) | copy-start | bytes 147460
  39.3 10.7 %all-to-all-start.2 = ((bf16[32,4,192]{2,1,0:T(4,128)(2,1)}), bf16[32,4,192]{2,1,0:T(4,128)(2,1)S(1)}, u32[]{:S(2)}, u32[]{:S(2)}) async-start(bf16[32,4,192]{2,1,0:T(4,128)(2,1)} %get-tuple-element.20), calls=%async_computation.2 | async-start | bytes 131072 | tf_op jit(solution)/shard_map/all_to_all | solution.py:187

commit v8 on v7

--- a/solution.py
+++ b/solution.py
@@ -66,28 +66,15 @@
     return dispatch, combine
 
 
-def slots_kernel(dims, tokens_hbm, out_grad_hbm, router_hbm, logits_out, sent, *scratch):
-    tokens, out_grad, router, sems = scratch
+def slots_kernel(dims, tokens, out_grad, router, logits_out, sent):
     n_expert, n_hidden, local_slots = dims
     images, _, width = tokens.shape
     place = places(orders(n_expert, n_hidden)[0])
-    copies = [
-        pltpu.make_async_copy(source, target, sems.at[i])
-        for i, (source, target) in enumerate(
-            ((tokens_hbm, tokens), (router_hbm, router), (out_grad_hbm, out_grad))
-        )
-    ]
-    for copy in copies:
-        copy.start()
-    copies[0].wait()
-    copies[1].wait()
     for image in range(images):
         logits = dot(router[...], tokens[image].T)
         logits_out[image] = logits
         dispatch, combine = softmaxes(logits)
         slot_in = dot(dispatch.astype(BF16), tokens[image]).astype(BF16)
-        if image == 0:
-            copies[2].wait()
         slot_grad = dot(combine.astype(BF16), out_grad[image]).astype(BF16)
         for expert in range(n_expert):
             own = slice(expert * local_slots, (expert + 1) * local_slots)
@@ -224,13 +211,6 @@
         ),
         tuple(pltpu.with_memory_space_constraint(x, pltpu.HBM) for x in (inputs, out_grads, router)),
         6 * images * slots * TOK * width,
-        in_specs=[pl.BlockSpec(memory_space=pltpu.HBM)] * 3,
-        scratch_shapes=[
-            pltpu.VMEM(inputs.shape, BF16),
-            pltpu.VMEM(out_grads.shape, BF16),
-            pltpu.VMEM(router.shape, BF16),
-            pltpu.SemaphoreType.DMA((3,)),
-        ],
     )
     (sent,) = call(
         lambda given, kept: None,

time: 51 us -> 50.9 us (level)
  no operation moved by 1% of the time
where the time goes in v8:
time: 50.9 us; the launch traced here: 50.7 us
  blocking collectives  33.9 us (67%)
  Pallas kernels  8.55 us (17%)
  starting transfers between devices  3.59 us (7%)
  waiting for transfers between devices  3.28 us (6%)
  between operations  0.7 us (1%)
  other arithmetic  0.64 us (1%)
    all_to_all x2, blocking collectives, exchange(): lax.all_to_all(blocks, BOTH, split_axis=0, concat_axis=0, tiled=True, axi...  33.9 us
    pallas_call x6, Pallas kernels, call(): pl.pallas_call(kernel, out_shape=outs, cost_estimate=pl.CostEstimate(flop...  8.55 us
    all_to_all x1, starting transfers between devices, exchange(): lax.all_to_all(blocks, BOTH, split_axis=0, concat_axis=0, tiled=True, axi...  3.59 us
    all_to_all x1, waiting for transfers between devices, exchange(): lax.all_to_all(blocks, BOTH, split_axis=0, concat_axis=0, tiled=True, axi...  3.28 us
  transfers between devices with their start and end apart: 1, of which 1 were waited for; matrix products, arithmetic and copies ran while one was open for 0% of the time, Pallas kernels for 8%

profile of v8, /device:TPU:0, one launch (start us, length us, event | category | flops | bytes accessed | tf_op | source)
XLA Modules:
  0.0 50.7 jit_solution(10920853478009206506)
XLA Ops:
  0.6 1.8 %shard_map.84 = (f32[1,32,196]{2,1,0:T(8,128)S(1)}, bf16[32,1,8,768]{3,2,1,0:T(8,128)(2,1)S(1)}) custom-call(bf16[1,196,768]{2,1,0:T(8,128)(2,1)} %bitcast.8, bf16[1,196,768]{2,1,0:T(8,128)(2,1)} %bitcast.10, bf16[32,768]{1,0:T(8,128)(2,1)} %bitcast.13), custom_call_target="tpu_custom_call" | custom-call | flops 28901376 | bytes 1069568 | tf_op jit(solution)/shard_map/pallas_call | solution.py:181
  2.4 0.0 copy-start
  2.4 0.0 copy-start.1
  2.4 20.1 %all_to_all.15.received = bf16[32,8,768]{2,1,0:T(8,128)(2,1)S(1)} all-to-all(bf16[32,8,768]{2,1,0:T(8,128)(2,1)S(1)} %bitcast.12), channel_id=1, replica_groups={{0,19,6,25,12,31,18,5,24,11,30,17,4,23,10,29,16,3,22,9,28,15,2,21,8,27,..., dimensions={0} | all-to-all | bytes 786432 | tf_op jit(solution)/shard_map/all_to_all | solution.py:174
  22.5 0.0 copy-done
  22.5 0.0 copy-done.1
  22.5 0.0 copy-start.2
  22.5 0.0 copy-start.3
  22.6 1.7 %shard_map.86 = (bf16[32,8,768]{2,1,0:T(8,128)(2,1)S(1)}, bf16[2,2,64,768]{3,2,1,0:T(8,128)(2,1)S(1)}, bf16[2,64,768]{2,1,0:T(8,128)(2,1)S(1)}, bf16[2,64,768]{2,1,0:T(8,128)(2,1)S(1)}) custom-call(bf16[32,8,768]{2,1,0:T(8,128)(2,1)S(1)} %all_to_all.15.received, bf16[2,768,768]{2,1,0:T(8,128)(2,1)S(1)} %copy-done, bf16[2,768,768]{2,1,0:T(8,128)(2,1)S(1)} %copy-done.1), custom_call_target="tpu_custom_call" | custom-call | flops 603979776 | bytes 6291456 | tf_op jit(solution)/shard_map/pallas_call | solution.py:181
  24.3 0.0 copy-start.4
  24.3 13.8 %all_to_all.16 = bf16[32,8,768]{2,1,0:T(8,128)(2,1)S(1)} all-to-all(bf16[32,8,768]{2,1,0:T(8,128)(2,1)S(1)} %get-tuple-element.17), channel_id=1, replica_groups={{0,19,2,17,4,23,6,21,8,27,10,25,12,31,14,29,16,3,18,1,20,7,22,5,24,11,2..., dimensions={0} | all-to-all | bytes 786432 | tf_op jit(solution)/shard_map/all_to_all | solution.py:174
  38.1 0.0 copy-done.2
  38.1 0.0 copy-done.3
  38.1 1.2 %shard_map.87 = (bf16[32,4,192]{2,1,0:T(4,128)(2,1)}, bf16[1,64,196]{2,1,0:T(8,128)(2,1)S(1)}, bf16[1,32,768]{2,1,0:T(8,128)(2,1)S(1)}) custom-call(f32[1,32,196]{2,1,0:T(8,128)S(1)} %get-tuple-element.15.logits_in, bf16[1,196,768]{2,1,0:T(8,128)(2,1)S(1)} %bitcast.9, bf16[1,196,768]{2,1,0:T(8,128)(2,1)S(1)} %bitcast.11, bf16[32,1,8,768]{3,2,1,0:T(8,128)(2,1)S(1)} %bitcast.7), custom_call_target="tpu_custom_call" | custom-call | flops 28901376 | bytes 1143808 | tf_op jit(solution)/shard_map/pallas_call | solution.py:181
  39.3 3.6 %all-to-all-start.2 = ((bf16[32,4,192]{2,1,0:T(4,128)(2,1)}), bf16[32,4,192]{2,1,0:T(4,128)(2,1)S(1)}, u32[]{:S(2)}, u32[]{:S(2)}) async-start(bf16[32,4,192]{2,1,0:T(4,128)(2,1)} %get-tuple-element.20), calls=%async_computation.2 | async-start | bytes 131072 | tf_op jit(solution)/shard_map/all_to_all | solution.py:174
  42.9 2.9 %shard_map.89 = (bf16[2,768,768]{2,1,0:T(8,128)(2,1)}, bf16[2,768,768]{2,1,0:T(8,128)(2,1)}) custom-call(bf16[2,2,64,768]{3,2,1,0:T(8,128)(2,1)S(1)} %get-tuple-element.21.rows, bf16[2,64,768]{2,1,0:T(8,128)(2,1)S(1)} %get-tuple-element.22.act, bf16[2,64,768]{2,1,0:T(8,128)(2,1)S(1)} %get-tuple-element.23.d_pre), custom_call_target="tpu_custom_call" | custom-call | flops 301989888 | bytes 5505024 | tf_op jit(solution)/shard_map/pallas_call | solution.py:181
  45.8 0.0 copy-done.4
  45.8 1.0 %shard_map.88 = bf16[1,196,768]{2,1,0:T(8,128)(2,1)} custom-call(bf16[1,64,196]{2,1,0:T(8,128)(2,1)S(1)} %get-tuple-element.18.left, bf16[1,32,768]{2,1,0:T(8,128)(2,1)S(1)} %get-tuple-element.19.slot_in_grad, bf16[32,768]{1,0:T(8,128)(2,1)S(1)} %bitcast.14), custom_call_target="tpu_custom_call" | custom-call | flops 19267584 | bytes 424448 | tf_op jit(solution)/shard_map/pallas_call | solution.py:181
  46.8 3.3 %all-to-all-done.2 = bf16[32,4,192]{2,1,0:T(4,128)(2,1)S(1)} async-done(((bf16[32,4,192]{2,1,0:T(4,128)(2,1)}), bf16[32,4,192]{2,1,0:T(4,128)(2,1)S(1)}, u32[]{:S(2)}, u32[]{:S(2)}) %all-to-all-start.2) | async-done | bytes 49184 | tf_op jit(solution)/shard_map/all_to_all | solution.py:174
  50.0 0.6 %convert_reduce_fusion = f32[4,192]{1,0:T(4,128)} fusion(bf16[32,4,192]{2,1,0:T(4,128)(2,1)S(1)} %all-to-all-done.2), kind=kLoop, calls=%fused_computation | loop fusion | flops 48384 | bytes 52224 | tf_op jit(solution)/shard_map/reduce_sum | solution.py:280
  (1 shorter events, 0.0 us)
Async XLA Ops:
  2.4 20.1 %copy-start = (bf16[2,768,768]{2,1,0:T(8,128)(2,1)S(1)}, bf16[2,768,768]{2,1,0:T(8,128)(2,1)}, u32[]{:S(2)}) copy-start(bf16[2,768,768]{2,1,0:T(8,128)(2,1)} %weight_in.1) | copy-start | bytes 7077892
  2.4 20.1 %copy-start.1 = (bf16[2,768,768]{2,1,0:T(8,128)(2,1)S(1)}, bf16[2,768,768]{2,1,0:T(8,128)(2,1)}, u32[]{:S(2)}) copy-start(bf16[2,768,768]{2,1,0:T(8,128)(2,1)} %weight_out.1) | copy-start | bytes 7077892
  22.5 15.6 %copy-start.2 = (bf16[196,768]{1,0:T(8,128)(2,1)S(1)}, bf16[196,768]{1,0:T(8,128)(2,1)}, u32[]{:S(2)}) copy-start(bf16[196,768]{1,0:T(8,128)(2,1)} %param.5) | copy-start | bytes 903172
  22.5 15.6 %copy-start.3 = (bf16[196,768]{1,0:T(8,128)(2,1)S(1)}, bf16[196,768]{1,0:T(8,128)(2,1)}, u32[]{:S(2)}) copy-start(bf16[196,768]{1,0:T(8,128)(2,1)} %param.6) | copy-start | bytes 903172
  24.3 21.5 %copy-start.4 = (bf16[768,32]{0,1:T(8,128)(2,1)S(1)}, bf16[768,32]{0,1:T(8,128)(2,1)}, u32[]{:S(2)}) copy-start(bf16[768,32]{0,1:T(8,128)(2,1)} %param.7) | copy-start | bytes 147460
  39.3 10.7 %all-to-all-start.2 = ((bf16[32,4,192]{2,1,0:T(4,128)(2,1)}), bf16[32,4,192]{2,1,0:T(4,128)(2,1)S(1)}, u32[]{:S(2)}, u32[]{:S(2)}) async-start(bf16[32,4,192]{2,1,0:T(4,128)(2,1)} %get-tuple-element.20), calls=%async_computation.2 | async-start | bytes 131072 | tf_op jit(solution)/shard_map/all_to_all | solution.py:174
